TPU v7x, 512 devices: a whole 4x8x8 slice. The times are simulated.
512 devices in a mesh: dp: 64 (over y, z), rep: 8 (over x, core).
Axes of the slice: x: 4, y: 8, z: 8, core: 2. Of those that a mesh axis runs over, the one named last changes fastest.
Arguments:
- tokens: bfloat16 [11264, 1280], P('dp'), may hold values from -6 to 6
- cotangent: bfloat16 [8192, 1280], P('dp'), may hold values from -16 to 16
- counts: int32 [64, 8], replicated, may hold values from 0 to 96, as said below
- hops: int32 [64, 8], replicated, may hold values from 0 to 3, as said below
- offsets: int32 [64, 8], replicated, may hold values from 0 to 128, as said below
- norm_gain: float32 [1280], replicated, may hold values from 0.1 to 1.9
- qkv_weight: bfloat16 [1280, 3840], P('dp', 'rep'), as said below
- out_weight: bfloat16 [1280, 1280], P('dp', 'rep'), may hold values from -0.15625 to 0.15625
Outputs:
- layer_out: bfloat16 [8192, 1280], P('dp')
- input_grad: bfloat16 [11264, 1280], P('dp')
- grad_qkv: float32 [1280, 3840], P('dp', 'rep')
- grad_out: float32 [1280, 1280], P('dp', 'rep')
- grad_gain: float32 [1280], P('dp')
Inputs may be any that keep to these rules, and one draw needn't show every extreme that they name: `counts`: the images of one dp index lie one after another from its first home row and take at most 176 rows; some dp index takes all 176. A slot may hold 0 patches. `hops`: every dp index has exactly two slots with each hop 0 to 3, in an order drawn from the seed. The images that one dp index sends at one hop hold at most 16 patches together and each at most half of 16; both bounds are reached. `offsets`: the images that arrive at a dp index, its own hop 0 images included, fill its 128 work rows exactly, without gaps or intersections. `qkv_weight`: columns head after head, each head's query, key and value columns in that order.
All inputs are finite; a program needn't handle non-finite values.
Results may differ from a plain program's by a relative error of at most 0.018.
Values may be sent and summed in bfloat16 or wider, within the bound.
A program may use at most 64 MiB of HBM per device.

v0:
```python
import jax
import jax.numpy as jnp
from jax import lax
from jax.sharding import PartitionSpec as P

HEAD = 80
REACH = 3


EPSILON = 1e-06
NEGATIVE = -1e30


def shifted(value, axis, steps):
    count = lax.axis_size(axis)
    pairs = [(source, (source + steps) % count) for source in range(count)]
    return lax.ppermute(value, axis, pairs)


def slot_tables(counts, hops):
    image_ends = jnp.cumsum(counts, axis=1)
    starts = image_ends - counts
    distances = jnp.arange(REACH + 1, dtype=jnp.int32)
    onehot = (hops[:, :, None] == distances[None, None, :]).astype(jnp.int32)
    per_hop = counts[:, :, None] * onehot
    before = jnp.cumsum(per_hop, axis=1) - per_hop
    within = jnp.sum(before * onehot, axis=2)
    return (starts, within)


def pick_rows(lower_row, length, source, size):
    position = jnp.arange(size, dtype=jnp.int32)[:, None]
    inside = (position >= lower_row[None, :]) & (position < (lower_row + length)[None, :])
    row_index = jnp.sum(
        jnp.where(inside, source[None, :] + position - lower_row[None, :], 0), axis=1
    )
    return (row_index, jnp.any(inside, axis=1), inside)


def route_tables(counts, hops, offsets, device, count_dp, home_rows, work_rows, slot_rows):
    starts, within = slot_tables(counts, hops)
    image_total = counts.shape[1]
    own_counts = counts[device]
    own_hops = hops[device]
    own_starts = starts[device]
    own_within = within[device]
    own_offsets = offsets[device]
    send_index, send_valid, back_index, back_valid = ([], [], [], [])
    work_lower, work_length, work_source, work_ident = ([], [], [], [])
    for distance in range(REACH + 1):
        sender = (device - distance) % count_dp
        sender_counts = counts[sender]
        sender_within = within[sender]
        sender_offsets = offsets[sender]
        length = jnp.where(hops[sender] == distance, sender_counts, 0)
        work_lower.append(sender_offsets)
        work_length.append(length)
        work_ident.append(sender * image_total + jnp.arange(image_total, dtype=jnp.int32))
        if distance == 0:
            work_source.append(starts[sender])
        else:
            work_source.append(home_rows + (distance - 1) * slot_rows + sender_within)
            own_length = jnp.where(own_hops == distance, own_counts, 0)
            forward_index, forward_valid, unused_forward = pick_rows(
                own_within, own_length, own_starts, slot_rows
            )
            backward_index, backward_valid, unused_backward = pick_rows(
                sender_within, length, sender_offsets, slot_rows
            )
            send_index.append(forward_index)
            send_valid.append(forward_valid)
            back_index.append(backward_index)
            back_valid.append(backward_valid)
    work_index, unused_valid, work_inside = pick_rows(
        jnp.concatenate(work_lower),
        jnp.concatenate(work_length),
        jnp.concatenate(work_source),
        work_rows,
    )
    work_image = jnp.sum(jnp.where(work_inside, jnp.concatenate(work_ident)[None, :], 0), axis=1)
    home_source = jnp.where(
        own_hops == 0, own_offsets, work_rows + (own_hops - 1) * slot_rows + own_within
    )
    home_index, home_valid, home_inside = pick_rows(own_starts, own_counts, home_source, home_rows)
    own_ident = device * image_total + jnp.arange(image_total, dtype=jnp.int32)
    home_image = jnp.sum(jnp.where(home_inside, own_ident[None, :], 0), axis=1)
    home_image = jnp.where(home_valid, home_image, -1 - jnp.arange(home_rows, dtype=jnp.int32))
    return (
        jnp.stack(send_index),
        jnp.stack(send_valid),
        jnp.stack(back_index),
        jnp.stack(back_valid),
        work_index,
        work_image,
        home_index,
        home_valid,
        home_image,
    )


def send_forward(slots):
    pieces = [shifted(slots[level], "dp", level + 1) for level in range(REACH)]
    return jnp.concatenate(pieces, axis=0)


def send_backward(slots):
    pieces = [shifted(slots[level], "dp", -(level + 1)) for level in range(REACH)]
    return jnp.concatenate(pieces, axis=0)


def to_work(home_array, tables):
    send_index, send_valid = (tables[0], tables[1])
    slots = jnp.where(send_valid[:, :, None], jnp.take(home_array, send_index, axis=0), 0)
    arrived = send_forward(slots)
    source = jnp.concatenate([home_array, arrived], axis=0)
    return jnp.take(source, tables[4], axis=0)


def to_home(work_array, tables):
    back_index, back_valid = (tables[2], tables[3])
    slots = jnp.where(back_valid[:, :, None], jnp.take(work_array, back_index, axis=0), 0)
    arrived = send_backward(slots)
    source = jnp.concatenate([work_array, arrived], axis=0)
    return jnp.where(tables[7][:, None], jnp.take(source, tables[6], axis=0), 0)


def norm_backward(grad_hidden, normed, inverse, upstream, norm_gain):
    grad_gain = jnp.sum(grad_hidden * normed, axis=0)
    grad_normed = grad_hidden * norm_gain
    correction = (
        grad_normed
        - jnp.mean(grad_normed, axis=1, keepdims=True)
        - normed * jnp.mean(grad_normed * normed, axis=1, keepdims=True)
    )
    work_grad = (upstream.astype(jnp.float32) + inverse * correction).astype(jnp.bfloat16)
    return (work_grad, grad_gain)


def encoder_layer(patch_rows, images, upstream, norm_gain, qkv_full, out_full):
    row_count = patch_rows.shape[0]
    head_count = qkv_full.shape[1] // (3 * HEAD)
    wide_rows = patch_rows.astype(jnp.float32)
    centred = wide_rows - jnp.mean(wide_rows, axis=1, keepdims=True)
    inverse = lax.rsqrt(jnp.mean(centred * centred, axis=1, keepdims=True) + EPSILON)
    normed = centred * inverse
    hidden = (normed * norm_gain).astype(jnp.bfloat16)
    projected_qkv = jnp.dot(hidden, qkv_full, preferred_element_type=jnp.float32).astype(
        jnp.bfloat16
    )
    projected_qkv = projected_qkv.reshape(row_count, head_count, 3, HEAD)
    queries = projected_qkv[:, :, 0]
    key_part = projected_qkv[:, :, 1]
    value_part = projected_qkv[:, :, 2]
    score_scale = HEAD ** (-0.5)
    same_image = images[:, None] == images[None, :]
    scores = (
        jnp.einsum("qhd,khd->hqk", queries, key_part, preferred_element_type=jnp.float32)
        * score_scale
    )
    scores = jnp.where(same_image[None], scores, NEGATIVE)
    row_max = jnp.max(scores, axis=2, keepdims=True)
    exponent = jnp.exp(scores - row_max)
    probs = exponent / jnp.sum(exponent, axis=2, keepdims=True)
    probs_low = probs.astype(jnp.bfloat16)
    attended = jnp.einsum(
        "hqk,khd->qhd", probs_low, value_part, preferred_element_type=jnp.float32
    ).astype(jnp.bfloat16)
    attended = attended.reshape(row_count, head_count * HEAD)
    piece = attended
    projected = lax.psum(
        lax.dot_general(
            piece, out_full, (((1,), (1,)), ((), ())), preferred_element_type=jnp.float32
        ).astype(jnp.bfloat16),
        "rep",
    ).astype(jnp.float32)
    layer_rows = (wide_rows + projected).astype(jnp.bfloat16)
    grad_attended = jnp.dot(upstream, out_full, preferred_element_type=jnp.float32).astype(
        jnp.bfloat16
    )
    grad_out = lax.dot_general(
        upstream, attended, (((0,), (0,)), ((), ())), preferred_element_type=jnp.float32
    )
    grad_heads = grad_attended.reshape(row_count, head_count, HEAD)
    grad_probs = jnp.einsum(
        "qhd,khd->hqk", grad_heads, value_part, preferred_element_type=jnp.float32
    )
    grad_values = jnp.einsum(
        "hqk,qhd->khd", probs_low, grad_heads, preferred_element_type=jnp.float32
    ).astype(jnp.bfloat16)
    grad_scores = probs * (grad_probs - jnp.sum(probs * grad_probs, axis=2, keepdims=True))
    grad_scores = (grad_scores * score_scale).astype(jnp.bfloat16)
    grad_queries = jnp.einsum(
        "hqk,khd->qhd", grad_scores, key_part, preferred_element_type=jnp.float32
    ).astype(jnp.bfloat16)
    grad_keys = jnp.einsum(
        "hqk,qhd->khd", grad_scores, queries, preferred_element_type=jnp.float32
    ).astype(jnp.bfloat16)
    grad_mixed = jnp.stack([grad_queries, grad_keys, grad_values], axis=2).reshape(
        row_count, head_count * 3 * HEAD
    )
    grad_qkv = lax.dot_general(
        hidden, grad_mixed, (((0,), (0,)), ((), ())), preferred_element_type=jnp.float32
    )
    piece = grad_mixed
    grad_hidden = lax.psum(
        lax.dot_general(
            piece, qkv_full, (((1,), (1,)), ((), ())), preferred_element_type=jnp.float32
        ).astype(jnp.bfloat16),
        "rep",
    ).astype(jnp.float32)
    work_grad, grad_gain = norm_backward(grad_hidden, normed, inverse, upstream, norm_gain)
    return (layer_rows, work_grad, grad_qkv, grad_out, grad_gain)


def body(tokens, cotangent, counts, hops, offsets, norm_gain, qkv_weight, out_weight):
    count_dp = lax.axis_size("dp")
    device = lax.axis_index("dp")
    home_rows = tokens.shape[0]
    work_rows = cotangent.shape[0]
    slot_rows = (home_rows - work_rows) // REACH
    qkv_full, out_full = (
        lax.all_gather(qkv_weight, "dp", axis=0, tiled=True),
        lax.all_gather(out_weight, "dp", axis=0, tiled=True),
    )
    tables = route_tables(counts, hops, offsets, device, count_dp, home_rows, work_rows, slot_rows)
    upstream = to_home(cotangent, tables)
    layer_rows, home_grad, grad_qkv, grad_out, grad_gain = encoder_layer(
        tokens, tables[8], upstream, norm_gain, qkv_full, out_full
    )
    layer_out = to_work(layer_rows, tables)
    grad_qkv, grad_out, grad_gain = (
        lax.psum_scatter(grad_qkv, "dp", scatter_dimension=0, tiled=True),
        lax.psum_scatter(grad_out, "dp", scatter_dimension=0, tiled=True),
        lax.psum_scatter(grad_gain, "dp", scatter_dimension=0, tiled=True),
    )
    return (layer_out, home_grad, grad_qkv, grad_out, grad_gain)


def solution(mesh):
    return jax.shard_map(
        body,
        mesh=mesh,
        in_specs=(P("dp", None), P("dp", None), P(), P(), P(), P(), P("dp", "rep"), P("dp", "rep")),
        out_specs=(P("dp", None), P("dp", None), P("dp", "rep"), P("dp", "rep"), P("dp")),
        check_vma=False,
    )
```

profile of v0, /device:TPU:1, one launch (start us, length us, event | category | flops | bytes accessed | tf_op | source)
XLA Modules:
  0.0 363.1 jit_solution(17789965071951852414)
XLA Ops:
  10.9 1.5 fusion.41
  12.9 1.8 gather_fusion.2
  14.8 14.4 %collective-permute-start.3 = (bf16[16,1280]{1,0:T(8,128)(2,1)S(1)}, bf16[16,1280]{1,0:T(8,128)(2,1)S(1)}, u32[]{:S(2)}, u32[]{:S(2)}) collective-permute-start(bf16[16,1280]{1,0:T(8,128)(2,1)S(1)} %get-tuple-element.49), channel_id=1, source_target_pairs={{0,504},{8,0},{16,8},{24,16},{32,24},{40,32},{48,40},{56,48},{64,5... | collective-permute-start | bytes 122888 | tf_op jit(solution)/shard_map/ppermute | solution.py:17
  29.3 2.2 collective-permute-start.5
  31.4 1.9 collective-permute-start.4
  36.5 40.1 %all-gather.1 = bf16[64,20,160]{2,1,0:T(8,128)(2,1)S(1)} all-gather(bf16[1,20,160]{2,1,0:T(8,128)(2,1)S(1)} %bitcast.130), channel_id=1, replica_groups=mesh['dp'=64,'rep'=8] {'dp'}, dimensions={0}, use_global_device_ids=true | all-gather | bytes 416000 | tf_op jit(solution)/shard_map/all_gather | solution.py:223
  77.1 1.0 gather_fusion.3
  78.6 17.6 %all-gather.4.cloned.1.call-done = bf16[64,20,480]{2,1,0:T(8,128)(2,1)} async-done(((bf16[1,20,480]{2,1,0:T(8,128)(2,1)}), bf16[64,20,480]{2,1,0:T(8,128)(2,1)}) %all-gather.4.cloned.1.call-update) | async-done | bytes 1228816 | tf_op jit(solution)/shard_map/all_gather | solution.py:222
  96.2 2.5 reshape.508
  99.4 1.1 fusion.91
  101.0 1.1 fusion.14
  102.1 1.1 fusion.36
  103.2 2.0 fusion.12
  105.2 2.0 fusion.13
  107.2 1.2 convolution_convert_fusion.1
  108.4 1.0 pad_maximum_fusion.2
  109.5 1.4 convolution_convert_fusion
  111.0 1.6 fusion.90
  112.6 2.2 fusion.87
  115.5 67.3 %all-reduce.10.cloned.1.call-done = (bf16[176,1280]{1,0:T(8,128)(2,1)}, bf16[176,1280]{1,0:T(8,128)(2,1)}) async-done(((bf16[176,1280]{1,0:T(8,128)(2,1)}, bf16[176,1280]{1,0:T(8,128)(2,1)}), (bf16[176,1280]{1,0:T(8,128)(2,1)}, bf16[176,1280]{1,0:T(8,128)(2,1)})) %all-reduce.10.cloned.1.call-update) | async-done | bytes 901136 | tf_op jit(solution)/shard_map/psum | solution.py:170
  182.8 1.5 fusion.26
  184.3 2.5 fusion.23
  187.6 2.7 collective-permute-start
  190.3 6.6 %collective-permute-start.2 = (bf16[16,1280]{1,0:T(8,128)(2,1)S(1)}, bf16[16,1280]{1,0:T(8,128)(2,1)S(1)}, u32[]{:S(2)}, u32[]{:S(2)}) collective-permute-start(bf16[16,1280]{1,0:T(8,128)(2,1)S(1)} %get-tuple-element.47), channel_id=1, source_target_pairs={{0,24},{8,32},{16,40},{24,48},{32,56},{40,64},{48,72},{56,80},{64,... | collective-permute-start | bytes 122888 | tf_op jit(solution)/shard_map/ppermute | solution.py:17
  196.9 2.6 collective-permute-start.1
  199.5 1.3 dynamic-slice
  201.4 117.5 %all-reduce.2 = f32[1280]{0:T(1024)S(1)} all-reduce(f32[1280]{0:T(1024)S(1)} %get-tuple-element.5), channel_id=4, replica_groups=mesh['dp'=64,'rep'=8] {'dp'}, use_global_device_ids=true, to_apply=%region_31.32.clone | all-reduce | flops 1280 | bytes 10240
  319.6 0.9 gather_fusion.1
  320.5 0.8 broadcast_select_fusion
  321.4 32.4 %all-reduce.8.cloned.1.call-done = (f32[1280,480]{1,0:T(8,128)}, f32[1280,160]{1,0:T(8,128)}) async-done(((f32[1280,480]{1,0:T(8,128)}, f32[1280,160]{1,0:T(8,128)}), (f32[1280,480]{1,0:T(8,128)}, f32[1280,160]{1,0:T(8,128)})) %all-reduce.8.cloned.1.call-update) | async-done | bytes 3276816
  353.7 1.5 constant_dynamic-slice_fusion.22
  355.2 1.4 constant_dynamic-slice_fusion.21
  (124 shorter events, 11.4 us)
Async XLA Ops:
  7.2 28.2 %copy-start = (bf16[176,1280]{1,0:T(8,128)(2,1)S(1)}, bf16[176,1280]{1,0:T(8,128)(2,1)}, u32[]{:S(2)}) copy-start(bf16[176,1280]{1,0:T(8,128)(2,1)} %param.8) | copy-start | bytes 1351684
  7.2 89.0 %all-gather.4.cloned.1.call-start = ((), (), s32[]{:S(2)}) async-start(), calls=%async_computation | async-start | bytes 1597440 | tf_op jit(solution)/shard_map/all_gather | solution.py:222
  7.9 174.9 %all-reduce.10.cloned.1.call-start = ((), (), s32[]{:S(2)}) async-start(), calls=%async_computation.2 | async-start | bytes 1802240 | tf_op jit(solution)/shard_map/psum | solution.py:170
  12.9 23.6 %copy-start.9 = (bf16[20,160]{1,0:T(8,128)(2,1)S(1)}, bf16[20,160]{1,0:T(8,128)(2,1)}, u32[]{:S(2)}) copy-start(bf16[20,160]{1,0:T(8,128)(2,1)} %param.15) | copy-start | bytes 19204
  14.8 62.1 %collective-permute-start.3 = (bf16[16,1280]{1,0:T(8,128)(2,1)S(1)}, bf16[16,1280]{1,0:T(8,128)(2,1)S(1)}, u32[]{:S(2)}, u32[]{:S(2)}) collective-permute-start(bf16[16,1280]{1,0:T(8,128)(2,1)S(1)} %get-tuple-element.49), channel_id=1, source_target_pairs={{0,504},{8,0},{16,8},{24,16},{32,24},{40,32},{48,40},{56,48},{64,5... | collective-permute-start | bytes 122888 | tf_op jit(solution)/shard_map/ppermute | solution.py:17
  29.3 47.7 %collective-permute-start.5 = (bf16[16,1280]{1,0:T(8,128)(2,1)S(1)}, bf16[16,1280]{1,0:T(8,128)(2,1)S(1)}, u32[]{:S(2)}, u32[]{:S(2)}) collective-permute-start(bf16[16,1280]{1,0:T(8,128)(2,1)S(1)} %get-tuple-element.50), channel_id=1, source_target_pairs={{0,488},{8,496},{16,504},{24,0},{32,8},{40,16},{48,24},{56,32},{64... | collective-permute-start | bytes 122888 | tf_op jit(solution)/shard_map/ppermute | solution.py:17
  31.4 45.6 %collective-permute-start.4 = (bf16[16,1280]{1,0:T(8,128)(2,1)S(1)}, bf16[16,1280]{1,0:T(8,128)(2,1)S(1)}, u32[]{:S(2)}, u32[]{:S(2)}) collective-permute-start(bf16[16,1280]{1,0:T(8,128)(2,1)S(1)} %get-tuple-element.51), channel_id=1, source_target_pairs={{0,496},{8,504},{16,0},{24,8},{32,16},{40,24},{48,32},{56,40},{64,... | collective-permute-start | bytes 122888 | tf_op jit(solution)/shard_map/ppermute | solution.py:17
  33.5 44.6 %copy-start.11 = (pred[176]{0:T(512)(128)(4,1)}, pred[176]{0:T(512)(128)(4,1)S(1)}, u32[]{:S(2)}) copy-start(pred[176]{0:T(512)(128)(4,1)S(1)} %fusion.40) | copy-start | bytes 532
  33.7 1.8 copy-start.13
  33.7 1.8 copy-start.15
  33.7 1.8 copy-start.17
  34.1 42.9 %copy-start.24 = (s32[128]{0:T(128)}, s32[128]{0:T(128)S(1)}, u32[]{:S(2)}) copy-start(s32[128]{0:T(128)S(1)} %select_reduce_fusion) | copy-start | bytes 1540
  35.6 63.2 %copy-start.5 = (f32[176]{0:T(256)}, f32[176]{0:T(256)S(1)}, u32[]{:S(2)}) copy-start(f32[176]{0:T(256)S(1)} %broadcast_multiply_fusion.2) | copy-start | bytes 2116
  35.6 41.4 %copy-start.1 = (bf16[128,1280]{1,0:T(8,128)(2,1)S(1)}, bf16[128,1280]{1,0:T(8,128)(2,1)}, u32[]{:S(2)}) copy-start(bf16[128,1280]{1,0:T(8,128)(2,1)} %param.9) | copy-start | bytes 983044
  36.4 41.7 %copy-start.19 = (pred[176]{0:T(512)(128)(4,1)}, pred[176]{0:T(512)(128)(4,1)S(1)}, u32[]{:S(2)}) copy-start(pred[176]{0:T(512)(128)(4,1)S(1)} %compare_and_fusion.1) | copy-start | bytes 532
  36.4 62.3 %copy-start.7 = (f32[176]{0:T(256)}, f32[176]{0:T(256)S(1)}, u32[]{:S(2)}) copy-start(f32[176]{0:T(256)S(1)} %add_rsqrt_fusion) | copy-start | bytes 2116
  78.6 22.3 %copy-start.2 = (bf16[176,160]{0,1:T(8,128)(2,1)}, bf16[176,160]{0,1:T(8,128)(2,1)S(1)}, u32[]{:S(2)}) copy-start(bf16[176,160]{0,1:T(8,128)(2,1)S(1)} %convolution_convert_fusion.3) | copy-start | bytes 168964
  78.6 20.2 %copy-start.3 = (f32[1280]{0:T(1024)S(1)}, f32[1280]{0:T(1024)}, u32[]{:S(2)}) copy-start(f32[1280]{0:T(1024)} %param.13) | copy-start | bytes 15364
  109.5 1.5 copy-start.12
  109.5 1.5 copy-start.20
  110.9 1.7 copy-start.4
  110.9 1.7 copy-start.6
  110.9 1.7 copy-start.8
  110.9 242.8 %all-reduce.8.cloned.1.call-start = ((), (), s32[]{:S(2)}) async-start(), calls=%async_computation.1 | async-start | bytes 7864320
  114.8 0.7 copy-start.21
  114.8 0.7 copy-start.23
  114.8 0.7 copy-start.25
  184.3 2.5 copy-start.10
  187.6 132.0 %collective-permute-start = (bf16[16,1280]{1,0:T(8,128)(2,1)S(1)}, bf16[16,1280]{1,0:T(8,128)(2,1)S(1)}, u32[]{:S(2)}, u32[]{:S(2)}) collective-permute-start(bf16[16,1280]{1,0:T(8,128)(2,1)S(1)} %get-tuple-element.46), channel_id=1, source_target_pairs={{0,8},{8,16},{16,24},{24,32},{32,40},{40,48},{48,56},{56,64},{64,7... | collective-permute-start | bytes 122888 | tf_op jit(solution)/shard_map/ppermute | solution.py:17
  190.3 129.3 %collective-permute-start.2 = (bf16[16,1280]{1,0:T(8,128)(2,1)S(1)}, bf16[16,1280]{1,0:T(8,128)(2,1)S(1)}, u32[]{:S(2)}, u32[]{:S(2)}) collective-permute-start(bf16[16,1280]{1,0:T(8,128)(2,1)S(1)} %get-tuple-element.47), channel_id=1, source_target_pairs={{0,24},{8,32},{16,40},{24,48},{32,56},{40,64},{48,72},{56,80},{64,... | collective-permute-start | bytes 122888 | tf_op jit(solution)/shard_map/ppermute | solution.py:17
  196.9 122.7 %collective-permute-start.1 = (bf16[16,1280]{1,0:T(8,128)(2,1)S(1)}, bf16[16,1280]{1,0:T(8,128)(2,1)S(1)}, u32[]{:S(2)}, u32[]{:S(2)}) collective-permute-start(bf16[16,1280]{1,0:T(8,128)(2,1)S(1)} %get-tuple-element.48), channel_id=1, source_target_pairs={{0,16},{8,24},{16,32},{24,40},{32,48},{40,56},{48,64},{56,72},{64,... | collective-permute-start | bytes 122888 | tf_op jit(solution)/shard_map/ppermute | solution.py:17
  319.6 0.9 copy-start.26
  (5 other events, 3.3 us)
Sparse Core Ops, SparseCore 0:
  11.1 85.1 all-gather.3
  111.0 71.6 all-reduce.9
  186.6 167.0 all-reduce.7
where the time goes:
time: 367 us; the launch traced here: 363 us
  blocking collectives  158 us (43%)
  waiting for transfers between devices  118 us (32%)
  starting transfers between devices  30.5 us (8%)
  between operations  15.1 us (4%)
  matrix products  15 us (4%)
  other arithmetic  13.8 us (4%)
  local copies, waits for them, and re-layouts  13.1 us (4%)
    unnamed x1, blocking collectives  118 us
    psum x1, waiting for transfers between devices, encoder_layer(): lax.psum(lax.dot_general(piece, out_full, (((1,), (1,)), ((), ())), prefe...  67.3 us
    all_gather x1, blocking collectives, body(): lax.all_gather(out_weight, 'dp', axis=0, tiled=True)  40.1 us
    unnamed x4, waiting for transfers between devices  33.1 us
    ppermute x6, starting transfers between devices, shifted(): return lax.ppermute(value, axis, pairs)  30.4 us
    all_gather x1, waiting for transfers between devices, body(): lax.all_gather(qkv_weight, 'dp', axis=0, tiled=True)  17.6 us
    unnamed x62, local copies, waits for them, and re-layouts  8.33 us
  transfers between devices with their start and end apart: 9, of which 3 were waited for; matrix products, arithmetic and copies ran while one was open for 7% of the time, Pallas kernels for 0%

commit v1 on v0

v1 whole, which is shorter than its diff:
```python
import jax
import jax.numpy as jnp
from jax import lax
from jax.experimental import pallas as pl
from jax.experimental.pallas import tpu as pltpu
from jax.sharding import PartitionSpec as P

MESH = pl.DeviceIdType.MESH
BF16 = jnp.bfloat16
F32 = jnp.float32

D = 1280
HEAD = 80
REACH = 3
SLOT = 16
WORK = 128
HOME = 176
SIDE = 8
REP = 8
ROWS = 20
GROUP = SIDE * ROWS
HALF = GROUP // 2
NEAR = SIDE // 2
IMAGES = 8
EPSILON = 1e-06
NEGATIVE = -1e30
PITCH = 24

TILES = (3, 2)
FIRST = (0, 384)
PACK = (80, 48)


def dot(a, b, ca=1, cb=0):
    return lax.dot_general(a, b, (((ca,), (cb,)), ((), ())), preferred_element_type=F32)


def onehot(match):
    return jnp.where(match, 1.0, 0.0).astype(BF16)


def iota(shape, dim):
    return lax.broadcasted_iota(jnp.int32, shape, dim)


def div20(v):
    return (v * 3277) >> 16


def images_of(counts, hops, offsets, dev):
    found = []
    start = jnp.int32(0)
    sent = [jnp.int32(0)] * (REACH + 1)
    for j in range(IMAGES):
        count, hop, offset = counts[dev, j], hops[dev, j], offsets[dev, j]
        within = jnp.int32(0)
        for level in range(1, REACH + 1):
            same = hop == level
            within = jnp.where(same, (level - 1) * SLOT + sent[level], within)
            sent[level] = sent[level] + jnp.where(same, count, 0)
        found.append((count, hop, offset, start, within))
        start = start + count
    return found


def spans_index(width, spans):
    lane = iota((1, width), 1)
    index = jnp.full((1, width), -1, jnp.int32)
    for lower, length, source in spans:
        inside = (lane >= lower) & (lane < lower + length)
        index = jnp.where(inside, lane + (source - lower), index)
    return index


def steps_of(direction):
    return [
        (distance, half)
        for distance in range(1, NEAR + 1)
        for half in (0, 1)
        if distance < NEAR or half == (1 if direction == 0 else 0)
    ]


STEPS = (steps_of(0), steps_of(1))


def kernel(
    tokens, cotangent, counts, hops, offsets, gain, qkv_w, out_w,
    layer_o, input_o, gq_o, go_o, gg_o,
    stage, own0, own1, parts0, parts1, w0, w1, pick0, pick1, put0, put1, perm,
    slots, arrived, work_s, normed_s, hidden_s, inv_s, both_s, both_t,
    g0, g1, ring0, ring1, back0, back1, heard0, heard1,
    hid_p, hid_r, lay_p, lay_r, work_g, lay_f, back_slots, back_arr, gain_s, gain_r,
    part_sem, ring_sem, token_sem, rep_sem, sum_sem, last_sem,
):
    d = lax.axis_index("dp")
    r = lax.axis_index("rep")
    y = d // SIDE
    z = d % SIDE

    def around(value, step, count):
        return lax.rem(value + (step + count), count)

    def at_y(step):
        return around(y, step, SIDE) * SIDE + z

    def at_z(step):
        return y * SIDE + around(z, step, SIDE)

    def at_dp(step):
        return around(d, step, SIDE * SIDE)

    def at_rep(step):
        return around(r, step, REP)

    pending = []

    def remote(src, dst, sems, dp, rep):
        return pltpu.make_async_remote_copy(
            src_ref=src, dst_ref=dst, send_sem=sems.at[0], recv_sem=sems.at[1],
            device_id=(dp, rep), device_id_type=MESH,
        )

    def send(copy):
        copy.start()
        pending.append(copy)
        return copy

    barrier = pltpu.get_barrier_semaphore()
    partners = (
        [(at_y(o), r) for o in range(1, SIDE)]
        + [(at_z(o), r) for o in range(1, SIDE)]
        + [(d, at_rep(o)) for o in range(1, REP)]
        + [(at_dp(o), r) for o in (1, 2, 3, -1, -2, -3)]
    )
    for partner in partners:
        pl.semaphore_signal(barrier, inc=1, device_id=partner, device_id_type=MESH)

    stage[...] = jnp.zeros_like(stage)
    wide = qkv_w[...].astype(F32)
    wide_out = out_w[...].astype(F32)
    for t in range(3):
        stage[PITCH * t : PITCH * t + ROWS, :] = wide[:, 128 * t : 128 * (t + 1)]
    own0[...] = stage[0 : PACK[0], :].astype(BF16)
    stage[0:ROWS, :] = jnp.concatenate([wide[:, 384:480], wide_out[:, 0:32]], axis=1)
    stage[PITCH : PITCH + ROWS, :] = wide_out[:, 32:160]
    own1[...] = stage[0 : PACK[1], :].astype(BF16)

    mine = images_of(counts, hops, offsets, d)
    out_index = spans_index(
        REACH * SLOT, [(w, jnp.where(h > 0, c, 0), s) for c, h, o, s, w in mine]
    )
    slots[...] = dot(
        onehot(iota((HOME, REACH * SLOT), 0) == out_index), tokens[...], 0, 0
    ).astype(BF16)

    pl.semaphore_wait(barrier, len(partners))

    own = (own0, own1)
    parts = (parts0, parts1)
    first_pos = (z, y)
    second_pos = (y, z)
    first_at = (at_z, at_y)
    second_at = (at_y, at_z)
    part_copies = []
    for o in range(1, SIDE):
        for s in (0, 1):
            part_copies.append(
                send(remote(own[s], parts[s].at[first_pos[s]], part_sem.at[s, o], first_at[s](o), r))
            )
    token_copies = [
        send(
            remote(
                slots.at[pl.ds(SLOT * (h - 1), SLOT)], arrived.at[pl.ds(SLOT * (h - 1), SLOT)],
                token_sem.at[0, h - 1], at_dp(h), r,
            )
        )
        for h in range(1, REACH + 1)
    ]
    for s in (0, 1):
        parts[s][first_pos[s]] = own[s][...]

    picks, puts = (pick0, pick1), (put0, put1)
    for s in (0, 1):
        rows = SIDE * PACK[s]
        lane = iota((1, rows), 1)
        block = (lane * 820) >> 16 if s == 0 else (lane * 1366) >> 16
        inner = lane - block * PACK[s]
        dense = iota((1, GROUP), 1)
        owner = div20(dense)
        for t in range(TILES[s]):
            row = inner - PITCH * t
            target = jnp.where((row >= 0) & (row < ROWS), block * ROWS + row, -1)
            picks[s][t] = onehot(iota((GROUP, rows), 0) == target)
            source = dense + owner * (PACK[s] - ROWS) + PITCH * t
            puts[s][t] = onehot(iota((rows, GROUP), 0) == source)

    work_spans, work_ids = [], []
    senders = [mine] + [
        images_of(counts, hops, offsets, at_dp(-h)) for h in range(1, REACH + 1)
    ]
    lane = iota((1, WORK), 1)
    ident = jnp.zeros((1, WORK), F32)
    for h, sender in enumerate(senders):
        for j, (c, hop, o, s, w) in enumerate(sender):
            length = jnp.where(hop == h, c, 0)
            work_spans.append((o, length, s if h == 0 else HOME + w))
            inside = (lane >= o) & (lane < o + length)
            ident = jnp.where(inside, float(h * IMAGES + j), ident)
    work_index = spans_index(WORK, work_spans)

    for copy in part_copies:
        copy.wait_recv()
    weights = (w0, w1)
    for s in (0, 1):
        block = parts[s][...].reshape(SIDE * PACK[s], 128)
        base = pl.multiple_of(second_pos[s] * GROUP, 16)
        for t in range(TILES[s]):
            weights[s][pl.ds(base, GROUP), 128 * t : 128 * (t + 1)] = dot(
                picks[s][t], block
            ).astype(BF16)

    def gather_copy(s, direction, distance, half):
        sign = 1 if direction == 0 else -1
        at = around(second_pos[s], -sign * (distance - 1), SIDE)
        rows = pl.ds(pl.multiple_of(at * GROUP + half * HALF, 16), HALF)
        number = STEPS[direction].index((distance, half))
        return remote(
            weights[s].at[rows], weights[s].at[rows],
            ring_sem.at[0, s, direction, number], second_at[s](sign), r,
        )

    def gather_step(distance):
        for half in (0, 1):
            for direction in (0, 1):
                if (distance, half) not in STEPS[direction]:
                    continue
                for s in (0, 1):
                    if distance > 1:
                        gather_copy(s, direction, distance - 1, half).wait_recv()
                    send(gather_copy(s, direction, distance, half))

    gather_step(1)

    for copy in token_copies:
        copy.wait_recv()
    work = dot(onehot(iota((HOME, WORK), 0) == work_index), tokens[...], 0, 0) + dot(
        onehot(iota((REACH * SLOT, WORK), 0) + HOME == work_index), arrived[...], 0, 0
    )
    work_s[...] = work.astype(BF16)
    centred = work - jnp.mean(work, axis=1, keepdims=True)
    inverse = lax.rsqrt(jnp.mean(centred * centred, axis=1, keepdims=True) + EPSILON)
    normed = centred * inverse
    normed_s[...] = normed
    inv_s[...] = jnp.broadcast_to(inverse, (WORK, 128))
    hidden_s[...] = (normed * gain[...]).astype(BF16)

    gather_step(2)

    lane = iota((1, D), 1)
    outer = (lane * 6554) >> 20
    inner = lane - outer * GROUP
    middle = div20(inner)
    natural = middle * GROUP + outer * ROWS + (inner - middle * ROWS)
    for b in range(D // 256):
        perm[256 * b : 256 * (b + 1), :] = onehot(iota((256, D), 0) + 256 * b == natural)
    gather_step(3)
    both_s[0:WORK, :] = dot(hidden_s[...], perm[...]).astype(BF16)
    both_s[WORK : 2 * WORK, :] = dot(cotangent[...], perm[...]).astype(BF16)
    gather_step(4)
    both_t[...] = both_s[...].astype(F32).T.astype(BF16)
    hidden_t = hidden_s[...].astype(F32).T.astype(BF16)
    ids = jnp.broadcast_to(ident, (WORK, WORK))
    same_image = ids == ids.T
    for direction in (0, 1):
        for distance, half in STEPS[direction]:
            if (distance + 1, half) not in STEPS[direction]:
                for s in (0, 1):
                    gather_copy(s, direction, distance, half).wait_recv()

    pa = dot(hidden_s[...], w0[...]).astype(BF16)
    pb = dot(both_s[...], w1[...]).astype(BF16)
    proj = jnp.concatenate([pa, pb[0:WORK, 0:128]], axis=1)
    scale = HEAD ** (-0.5)
    pieces, attended = [], []
    for j in (0, 1):
        q, k, v = (
            proj[:, 240 * j + HEAD * i : 240 * j + HEAD * (i + 1)] for i in range(3)
        )
        da = pb[WORK : 2 * WORK, 96 + HEAD * j : 96 + HEAD * (j + 1)]
        scores = jnp.where(same_image, dot(q, k, 1, 1) * scale, NEGATIVE)
        exponent = jnp.exp(scores - jnp.max(scores, axis=1, keepdims=True))
        probs = exponent / jnp.sum(exponent, axis=1, keepdims=True)
        probs_low = probs.astype(BF16)
        attended.append(dot(probs_low, v).astype(BF16))
        grad_probs = dot(da, v, 1, 1)
        grad_v = dot(probs_low, da, 0, 0).astype(BF16)
        grad_s = probs * (grad_probs - jnp.sum(probs * grad_probs, axis=1, keepdims=True))
        grad_s = (grad_s * scale).astype(BF16)
        pieces += [
            dot(grad_s, k).astype(BF16),
            dot(grad_s, q, 0, 0).astype(BF16),
            grad_v,
        ]
    mixed = jnp.concatenate(pieces + attended, axis=1)
    mix0 = mixed[:, 0:384]
    mix1 = mixed[:, 384:640]
    in_qkv = iota((WORK, 256), 1) < 96
    mix1_qkv = jnp.where(in_qkv, mix1, jnp.zeros_like(mix1))
    mix1_att = jnp.where(in_qkv, jnp.zeros_like(mix1), mix1)

    g0[...] = dot(hidden_t, mix0)
    g1[...] = dot(both_t[...], jnp.concatenate([mix1_qkv, mix1_att], axis=0))
    totals = (g0, g1)
    rings = (ring0, ring1)

    def sum_copy(s, direction, distance, half):
        sign = 1 if direction == 0 else -1
        number = STEPS[direction].index((distance, half))
        return remote(
            rings[s].at[direction, distance, half], rings[s].at[direction, distance - 1, half],
            ring_sem.at[1, s, direction, number], second_at[s](sign), r,
        )

    def own_term(s, step, half):
        at = around(second_pos[s], step, SIDE)
        return totals[s][pl.ds(pl.multiple_of(at * GROUP + half * HALF, 16), HALF), :]

    def sum_step(distance):
        for half in (0, 1):
            for direction in (0, 1):
                if (distance, half) not in STEPS[direction]:
                    continue
                sign = 1 if direction == 0 else -1
                for s in (0, 1):
                    total = own_term(s, sign * distance, half)
                    if (distance + 1, half) in STEPS[direction]:
                        sum_copy(s, direction, distance + 1, half).wait_recv()
                        total = total + rings[s][direction, distance, half].astype(F32)
                    rings[s][direction, distance, half] = total.astype(BF16)
                    send(sum_copy(s, direction, distance, half))

    def spread(kind, src, dst):
        copies = []
        for o in range(1, REP):
            rows = pl.ds(pl.multiple_of(at_rep(o) * 16, 16), 16)
            copies.append(
                send(remote(src.at[rows], dst.at[r], rep_sem.at[kind, o], d, at_rep(o)))
            )
        return copies

    my_rows = pl.ds(pl.multiple_of(r * 16, 16), 16)

    def summed(copies, src, dst):
        dst[r] = src[my_rows, :]
        for copy in copies:
            copy.wait_recv()
        total = dst[0].astype(F32)
        for i in range(1, REP):
            total = total + dst[i].astype(F32)
        return total

    def share(kind, ref):
        return [
            send(remote(ref.at[my_rows], ref.at[my_rows], rep_sem.at[kind, o], d, at_rep(o)))
            for o in range(1, REP)
        ]

    sum_step(4)
    turned = dot(mix1_qkv, w1[...], 1, 1).astype(BF16)
    hid_p[...] = (dot(mix0, w0[...], 1, 1) + dot(turned, perm[...])).astype(BF16)
    hid_copies = spread(0, hid_p, hid_r)
    sum_step(3)
    turned = dot(mix1_att, w1[...], 1, 1).astype(BF16)
    lay_p[...] = dot(turned, perm[...]).astype(BF16)
    lay_copies = spread(1, lay_p, lay_r)

    back_index = spans_index(
        REACH * SLOT,
        [
            (w, jnp.where(hop == h, c, 0), o)
            for h in range(1, REACH + 1)
            for c, hop, o, s, w in senders[h]
        ],
    )
    home_index = spans_index(
        HOME, [(s, c, jnp.where(h == 0, o, WORK + w)) for c, h, o, s, w in mine]
    )

    sum_step(2)
    grad_hidden = summed(hid_copies, hid_p, hid_r)
    norm_rows = normed_s[my_rows, :]
    grad_normed = grad_hidden * gain[...]
    correction = (
        grad_normed
        - jnp.mean(grad_normed, axis=1, keepdims=True)
        - norm_rows * jnp.mean(grad_normed * norm_rows, axis=1, keepdims=True)
    )
    work_g[my_rows, :] = (
        cotangent[my_rows, :].astype(F32) + inv_s[my_rows, 0:1] * correction
    ).astype(BF16)
    work_copies = share(2, work_g)

    sum_step(1)
    projected = summed(lay_copies, lay_p, lay_r)
    lay_f[my_rows, :] = (work_s[my_rows, :].astype(F32) + projected).astype(BF16)
    layer_copies = share(3, lay_f)

    for copy in work_copies:
        copy.wait_recv()
    back_slots[...] = dot(
        onehot(iota((WORK, REACH * SLOT), 0) == back_index), work_g[...], 0, 0
    ).astype(BF16)
    back_copies = [
        send(
            remote(
                back_slots.at[pl.ds(SLOT * (h - 1), SLOT)], back_arr.at[pl.ds(SLOT * (h - 1), SLOT)],
                token_sem.at[1, h - 1], at_dp(-h), r,
            )
        )
        for h in range(1, REACH + 1)
    ]

    backs, heards = (back0, back1), (heard0, heard1)
    last_copies = ([], [])
    for s in (0, 1):
        halves = []
        for half in (0, 1):
            total = own_term(s, 0, half)
            for direction in (0, 1):
                sum_copy(s, direction, 1, half).wait_recv()
                total = total + rings[s][direction, 0, half].astype(F32)
            halves.append(total.astype(BF16))
        dense = jnp.concatenate(halves, axis=0)
        spreadout = dot(puts[s][0], dense[:, 0:128])
        for t in range(1, TILES[s]):
            spreadout = spreadout + dot(puts[s][t], dense[:, 128 * t : 128 * (t + 1)])
        backs[s][...] = spreadout.astype(BF16).reshape(SIDE, PACK[s], 128)
        for o in range(1, SIDE):
            to = around(first_pos[s], o, SIDE)
            last_copies[s].append(
                send(remote(backs[s].at[to], heards[s].at[first_pos[s]], part_sem.at[2 + s, o], first_at[s](o), r))
            )
        heards[s][first_pos[s]] = backs[s][first_pos[s]]

    gain_at = iota((ROWS, D), 0) + d * ROWS == iota((ROWS, D), 1)
    own_gain = jnp.sum(jnp.where(gain_at, gain[...], 0.0), axis=1, keepdims=True)

    for copy in back_copies:
        copy.wait_recv()
    input_o[...] = (
        dot(onehot(iota((WORK, HOME), 0) == home_index), work_g[...], 0, 0)
        + dot(onehot(iota((REACH * SLOT, HOME), 0) + WORK == home_index), back_arr[...], 0, 0)
    ).astype(BF16)
    for copy in layer_copies:
        copy.wait_recv()
    layer_o[...] = lay_f[...]

    tiles = []
    for s in (0, 1):
        for copy in last_copies[s]:
            copy.wait_recv()
        total = heards[s][0].astype(F32)
        for i in range(1, SIDE):
            total = total + heards[s][i].astype(F32)
        tiles += [total[PITCH * t : PITCH * t + ROWS, :] for t in range(TILES[s])]
    grad_qkv = jnp.concatenate(tiles[0:3] + [tiles[3][:, 0:96]], axis=1)
    gq_o[...] = grad_qkv
    go_o[...] = jnp.concatenate([tiles[3][:, 96:128], tiles[4]], axis=1)
    share_gain = jnp.sum(grad_qkv * qkv_w[...].astype(F32), axis=1, keepdims=True) / own_gain
    gain_s[...] = jnp.zeros_like(gain_s)
    gain_s[0:ROWS, :] = jnp.broadcast_to(share_gain, (ROWS, 128))
    gain_copies = [
        send(remote(gain_s, gain_r.at[r], sum_sem.at[o], d, at_rep(o)))
        for o in range(1, REP)
    ]
    gain_r[r] = gain_s[...]
    for copy in gain_copies:
        copy.wait_recv()
    total = gain_r[0]
    for i in range(1, REP):
        total = total + gain_r[i]
    diagonal = iota((24, 128), 0) == iota((24, 128), 1)
    gg_o[...] = jnp.sum(jnp.where(diagonal, total, 0.0), axis=0, keepdims=True)[:, 0:ROWS]

    for copy in pending:
        copy.wait_send()


def body(tokens, cotangent, counts, hops, offsets, norm_gain, qkv_weight, out_weight):
    vmem = pl.BlockSpec(memory_space=pltpu.VMEM)
    smem = pl.BlockSpec(memory_space=pltpu.SMEM)
    dma = pltpu.SemaphoreType.DMA
    low = lambda *shape: pltpu.VMEM(shape, BF16)
    wide = lambda *shape: pltpu.VMEM(shape, F32)
    outs = pl.pallas_call(
        kernel,
        out_shape=(
            jax.ShapeDtypeStruct((WORK, D), BF16),
            jax.ShapeDtypeStruct((HOME, D), BF16),
            jax.ShapeDtypeStruct((ROWS, 480), F32),
            jax.ShapeDtypeStruct((ROWS, 160), F32),
            jax.ShapeDtypeStruct((1, ROWS), F32),
        ),
        in_specs=[vmem, vmem, smem, smem, smem, vmem, vmem, vmem],
        out_specs=(vmem,) * 5,
        scratch_shapes=[
            wide(80, 128),
            low(PACK[0], 128), low(PACK[1], 128),
            low(SIDE, PACK[0], 128), low(SIDE, PACK[1], 128),
            low(D, 384), low(D, 256),
            low(3, GROUP, SIDE * PACK[0]), low(2, GROUP, SIDE * PACK[1]),
            low(3, SIDE * PACK[0], GROUP), low(2, SIDE * PACK[1], GROUP),
            low(D, D),
            low(REACH * SLOT, D), low(REACH * SLOT, D),
            low(WORK, D), wide(WORK, D), low(WORK, D), wide(WORK, 128),
            low(2 * WORK, D), low(D, 2 * WORK),
            wide(D, 384), wide(D, 256),
            low(2, NEAR + 1, 2, HALF, 384), low(2, NEAR + 1, 2, HALF, 256),
            low(SIDE, PACK[0], 128), low(SIDE, PACK[1], 128),
            low(SIDE, PACK[0], 128), low(SIDE, PACK[1], 128),
            low(WORK, D), low(REP, 16, D), low(WORK, D), low(REP, 16, D),
            low(WORK, D), low(WORK, D),
            low(REACH * SLOT, D), low(REACH * SLOT, D),
            wide(24, 128), wide(REP, 24, 128),
            dma((4, SIDE, 2)),
            dma((2, 2, 2, 7, 2)),
            dma((2, REACH, 2)),
            dma((4, REP, 2)),
            dma((REP, 2)),
            dma((1,)),
        ],
        compiler_params=pltpu.CompilerParams(
            collective_id=0, has_side_effects=True, vmem_limit_bytes=50 * 1024 * 1024
        ),
        name="layer",
    )(
        tokens, cotangent, counts, hops, offsets,
        norm_gain.reshape(1, D), qkv_weight, out_weight,
    )
    layer_out, input_grad, grad_qkv, grad_out, grad_gain = outs
    return (layer_out, input_grad, grad_qkv, grad_out, grad_gain.reshape(ROWS))


def solution(mesh):
    return jax.shard_map(
        body,
        mesh=mesh,
        in_specs=(P("dp", None), P("dp", None), P(), P(), P(), P(), P("dp", "rep"), P("dp", "rep")),
        out_specs=(P("dp", None), P("dp", None), P("dp", "rep"), P("dp", "rep"), P("dp")),
        check_vma=False,
    )
```

time: 367 us -> 90.2 us (0.25)
  blocking collectives: 158 us -> 0 us
  waiting for transfers between devices: 118 us -> 0 us
  Pallas kernels: 0 us -> 81.1 us
  starting transfers between devices: 30.5 us -> 0 us
  matrix products: 15 us -> 0 us
  between operations: 15.1 us -> 0.66 us
  other arithmetic: 13.8 us -> 0 us
  local copies, waits for them, and re-layouts: 13.1 us -> 8.04 us
    unnamed x1 -> x0, blocking collectives: 118 us -> none
    pallas_call x0 -> x1, Pallas kernels: none -> 81.1 us  [body(): pl.pallas_call(kernel, out_shape=(jax.ShapeDtypeStruct((WORK, D), BF16),...]
    psum x1 -> x0, waiting for transfers between devices: 67.3 us -> none  [encoder_layer(): lax.psum(lax.dot_general(piece, out_full, (((1,), (1,)), ((), ())), prefe...]
    all_gather x1 -> x0, blocking collectives: 40.1 us -> none  [body(): lax.all_gather(out_weight, 'dp', axis=0, tiled=True)]
    unnamed x4 -> x0, waiting for transfers between devices: 33.1 us -> none
    ppermute x6 -> x0, starting transfers between devices: 30.4 us -> none  [shifted(): return lax.ppermute(value, axis, pairs)]
    all_gather x1 -> x0, waiting for transfers between devices: 17.6 us -> none  [body(): lax.all_gather(qkv_weight, 'dp', axis=0, tiled=True)]
    dot_general x11 -> x0, matrix products: 13.9 us -> none  [the longest x1 2.19 us: encoder_layer(): lax.dot_general(hidden, grad_mixed, (((0,), (0,)), ((), ())), preferred_e...]
  transfers between devices with their start and end apart: 9 -> 0, of which waited for: 3 -> 0; matrix products, arithmetic and copies ran while one was open for 7% -> 0% of each run, Pallas kernels for 0% -> 0%
where the time goes in v1:
time: 90.2 us; the launch traced here: 89.8 us
  Pallas kernels  81.1 us (90%)
  local copies, waits for them, and re-layouts  8.04 us (9%)
    pallas_call x1, Pallas kernels, body(): pl.pallas_call(kernel, out_shape=(jax.ShapeDtypeStruct((WORK, D), BF16),...  81.1 us
    unnamed x22, local copies, waits for them, and re-layouts  7.33 us

profile of v1, /device:TPU:1, one launch (start us, length us, event | category | flops | bytes accessed | tf_op | source)
XLA Modules:
  0.0 89.8 jit_solution(1465816126799976312)
XLA Ops:
  0.6 0.0 copy-start.4
  0.6 0.7 reshape.16.gain
  1.3 0.0 copy-done.4
  1.4 0.0 copy-start.5
  1.4 0.1 copy.13.counts
  1.4 0.6 copy-done.5
  2.0 0.0 copy-start.6
  2.0 0.1 copy.14.hops
  2.1 0.6 copy-done.6
  2.7 0.0 copy-start.2
  2.7 0.0 copy-start.3
  2.7 0.1 copy.15.offsets
  2.8 0.6 copy-done.2
  3.5 0.0 copy-done.3
  3.5 0.0 copy-start
  3.5 1.0 %copy-done = bf16[176,1280]{1,0:T(8,128)(2,1)S(1)} copy-done((bf16[176,1280]{1,0:T(8,128)(2,1)S(1)}, bf16[176,1280]{1,0:T(8,128)(2,1)}, u32[]{:S(2)}) %copy-start) | copy-done | bytes 450584
  4.5 0.0 copy-start.1
  4.5 1.0 %copy-done.1 = bf16[128,1280]{1,0:T(8,128)(2,1)S(1)} copy-done((bf16[128,1280]{1,0:T(8,128)(2,1)S(1)}, bf16[128,1280]{1,0:T(8,128)(2,1)}, u32[]{:S(2)}) %copy-start.1) | copy-done | bytes 327704
  5.5 81.1 %layer.1 = (bf16[128,1280]{1,0:T(8,128)(2,1)S(1)}, bf16[176,1280]{1,0:T(8,128)(2,1)S(1)}, f32[20,480]{1,0:T(8,128)S(1)}, f32[20,160]{1,0:T(8,128)S(1)}, f32[1,20]{1,0:T(1,128)S(1)}) custom-call(bf16[176,1280]{1,0:T(8,128)(2,1)S(1)} %copy-done, bf16[128,1280]{1,0:T(8,128)(2,1)S(1)} %copy-done.1, s32[64,8]{1,0:T(8,128)S(1)} %copy.13.counts, ...), custom_call_target="tpu_custom_call" | custom-call | tf_op jit(solution)/shard_map/layer/pallas_call | solution.py:496
  86.6 0.7 copy.21
  87.3 0.8 copy.22
  88.1 0.6 copy.23
  88.7 0.6 copy.24
  89.3 0.5 copy.25
Async XLA Ops:
  0.6 0.7 copy-start.4
  1.4 0.7 copy-start.5
  2.0 0.7 copy-start.6
  2.7 0.7 copy-start.2
  2.7 0.7 copy-start.3
  3.5 1.0 %copy-start = (bf16[176,1280]{1,0:T(8,128)(2,1)S(1)}, bf16[176,1280]{1,0:T(8,128)(2,1)}, u32[]{:S(2)}) copy-start(bf16[176,1280]{1,0:T(8,128)(2,1)} %tokens.1) | copy-start | bytes 1351684
  4.5 1.0 %copy-start.1 = (bf16[128,1280]{1,0:T(8,128)(2,1)S(1)}, bf16[128,1280]{1,0:T(8,128)(2,1)}, u32[]{:S(2)}) copy-start(bf16[128,1280]{1,0:T(8,128)(2,1)} %cotangent.1) | copy-start | bytes 983044

commit v2 on v1

v2 whole, which is shorter than its diff:
```python
import jax
import jax.numpy as jnp
from jax import lax
from jax.experimental import pallas as pl
from jax.experimental.pallas import tpu as pltpu
from jax.sharding import PartitionSpec as P

MESH = pl.DeviceIdType.MESH
BF16 = jnp.bfloat16
F32 = jnp.float32

D = 1280
HEAD = 80
REACH = 3
SLOT = 16
WORK = 128
HOME = 176
SIDE = 8
REP = 8
ROWS = 20
GROUP = SIDE * ROWS
NEAR = SIDE // 2
IMAGES = 8
EPSILON = 1e-06
NEGATIVE = -1e30
PITCH = 24

TILES = (3, 2)
FIRST = (0, 384)
PACK = (80, 48)


def dot(a, b, ca=1, cb=0):
    return lax.dot_general(a, b, (((ca,), (cb,)), ((), ())), preferred_element_type=F32)


def onehot(match):
    return jnp.where(match, 1.0, 0.0).astype(BF16)


def iota(shape, dim):
    return lax.broadcasted_iota(jnp.int32, shape, dim)


def div20(v):
    return (v * 3277) >> 16


def images_of(counts, hops, offsets, dev):
    found = []
    start = jnp.int32(0)
    sent = [jnp.int32(0)] * (REACH + 1)
    for j in range(IMAGES):
        count, hop, offset = counts[j, dev], hops[j, dev], offsets[j, dev]
        within = jnp.int32(0)
        for level in range(1, REACH + 1):
            same = hop == level
            within = jnp.where(same, (level - 1) * SLOT + sent[level], within)
            sent[level] = sent[level] + jnp.where(same, count, 0)
        found.append((count, hop, offset, start, within))
        start = start + count
    return found


def spans_index(width, spans):
    lane = iota((1, width), 1)
    index = jnp.full((1, width), -1, jnp.int32)
    for lower, length, source in spans:
        inside = (lane >= lower) & (lane < lower + length)
        index = jnp.where(inside, lane + (source - lower), index)
    return index


FAR = (((80, 48), (128, 32)), ((0, 48), (48, 32)))
PIECES = (FAR[0] + ((0, 80),), FAR[1] + ((80, 80),))


def steps_of(direction):
    return [
        (distance, piece)
        for distance in range(1, NEAR + 1)
        for piece in PIECES[direction]
        if distance < NEAR or piece in FAR[direction]
    ]


STEPS = (steps_of(0), steps_of(1))


def kernel(
    tokens_h, cotangent_h, counts_h, hops_h, offsets_h, gain_h, qkv_h, out_h,
    layer_h, input_h, gq_h, go_h, gg_h,
    tokens, cotangent, counts, hops, offsets, gain_v, qkv_w, out_w,
    input_o, gq_o, go_o, gg_o,
    stage, own0, own1, parts0, parts1, w0, w1, pick0, pick1, put0, put1, perm,
    slots, arrived, work_s, normed_s, hidden_s, inv_s, both_s, both_t,
    g0, g1, ring0, ring1, back0, back1, heard0, heard1,
    hid_p, hid_r, lay_p, lay_r, work_g, lay_f, back_slots, back_arr, gain_s, gain_r,
    part_sem, ring_sem, token_sem, rep_sem, sum_sem, in_sem, out_sem,
):
    d = lax.axis_index("dp")
    r = lax.axis_index("rep")
    y = d // SIDE
    z = d % SIDE

    def around(value, step, count):
        return lax.rem(value + (step + count), count)

    def at_y(step):
        return around(y, step, SIDE) * SIDE + z

    def at_z(step):
        return y * SIDE + around(z, step, SIDE)

    def at_dp(step):
        return around(d, step, SIDE * SIDE)

    def at_rep(step):
        return around(r, step, REP)

    sent = {}

    def remote(src, dst, sems, dp, rep):
        return pltpu.make_async_remote_copy(
            src_ref=src, dst_ref=dst, send_sem=sems.at[0], recv_sem=sems.at[1],
            device_id=(dp, rep), device_id_type=MESH,
        )

    def send(key, copy):
        copy.start()
        sent[key] = copy

    def got(key):
        sent[key].wait_recv()

    barrier = pltpu.get_barrier_semaphore()
    partners = (
        [(at_y(o), r) for o in range(1, SIDE)]
        + [(at_z(o), r) for o in range(1, SIDE)]
        + [(d, at_rep(o)) for o in range(1, REP)]
        + [(at_dp(o), r) for o in (1, 2, 3, -1, -2, -3)]
    )
    for partner in partners:
        pl.semaphore_signal(barrier, inc=1, device_id=partner, device_id_type=MESH)

    loads = [
        pltpu.make_async_copy(src, dst, in_sem.at[i])
        for i, (src, dst) in enumerate(
            (
                (qkv_h, qkv_w), (out_h, out_w), (counts_h, counts), (hops_h, hops),
                (offsets_h, offsets), (tokens_h, tokens), (gain_h, gain_v), (cotangent_h, cotangent),
            )
        )
    ]
    for load in loads:
        load.start()

    stage[...] = jnp.zeros_like(stage)
    for load in loads[0:2]:
        load.wait()
    wide = qkv_w[...].astype(F32)
    wide_out = out_w[...].astype(F32)
    for t in range(3):
        stage[PITCH * t : PITCH * t + ROWS, :] = wide[:, 128 * t : 128 * (t + 1)]
    own0[...] = stage[0 : PACK[0], :].astype(BF16)
    stage[0:ROWS, :] = jnp.concatenate([wide[:, 384:480], wide_out[:, 0:32]], axis=1)
    stage[PITCH : PITCH + ROWS, :] = wide_out[:, 32:160]
    own1[...] = stage[0 : PACK[1], :].astype(BF16)

    pl.semaphore_wait(barrier, len(partners))

    own = (own0, own1)
    parts = (parts0, parts1)
    first_pos = (z, y)
    second_pos = (y, z)
    first_at = (at_z, at_y)
    second_at = (at_y, at_z)
    for o in range(1, SIDE):
        for s in (0, 1):
            send(
                ("part", s, o),
                remote(own[s], parts[s].at[first_pos[s]], part_sem.at[s, o], first_at[s](o), r),
            )
    for load in loads[2:6]:
        load.wait()
    mine = images_of(counts, hops, offsets, d)
    out_index = spans_index(
        REACH * SLOT, [(w, jnp.where(h > 0, c, 0), s) for c, h, o, s, w in mine]
    )
    slots[...] = dot(
        onehot(iota((HOME, REACH * SLOT), 0) == out_index), tokens[...], 0, 0
    ).astype(BF16)
    for h in range(1, REACH + 1):
        rows = pl.ds(SLOT * (h - 1), SLOT)
        send(
            ("token", h),
            remote(slots.at[rows], arrived.at[rows], token_sem.at[0, h - 1], at_dp(h), r),
        )
    for s in (0, 1):
        parts[s][first_pos[s]] = own[s][...]

    picks, puts = (pick0, pick1), (put0, put1)
    for s in (0, 1):
        rows = SIDE * PACK[s]
        lane = iota((1, rows), 1)
        block = (lane * 820) >> 16 if s == 0 else (lane * 1366) >> 16
        inner = lane - block * PACK[s]
        dense = iota((1, GROUP), 1)
        owner = div20(dense)
        for t in range(TILES[s]):
            row = inner - PITCH * t
            target = jnp.where((row >= 0) & (row < ROWS), block * ROWS + row, -1)
            picks[s][t] = onehot(iota((GROUP, rows), 0) == target)
            source = dense + owner * (PACK[s] - ROWS) + PITCH * t
            puts[s][t] = onehot(iota((rows, GROUP), 0) == source)

    work_spans, work_ids = [], []
    senders = [mine] + [
        images_of(counts, hops, offsets, at_dp(-h)) for h in range(1, REACH + 1)
    ]
    lane = iota((1, WORK), 1)
    ident = jnp.zeros((1, WORK), F32)
    for h, sender in enumerate(senders):
        for j, (c, hop, o, s, w) in enumerate(sender):
            length = jnp.where(hop == h, c, 0)
            work_spans.append((o, length, s if h == 0 else HOME + w))
            inside = (lane >= o) & (lane < o + length)
            ident = jnp.where(inside, float(h * IMAGES + j), ident)
    work_index = spans_index(WORK, work_spans)

    for o in range(1, SIDE):
        for s in (0, 1):
            got(("part", s, o))
    weights = (w0, w1)
    for s in (0, 1):
        block = parts[s][...].reshape(SIDE * PACK[s], 128)
        base = pl.multiple_of(second_pos[s] * GROUP, 16)
        for t in range(TILES[s]):
            weights[s][pl.ds(base, GROUP), 128 * t : 128 * (t + 1)] = dot(
                picks[s][t], block
            ).astype(BF16)

    def gather_copy(s, direction, distance, piece):
        sign = 1 if direction == 0 else -1
        at = around(second_pos[s], -sign * (distance - 1), SIDE)
        rows = pl.ds(pl.multiple_of(at * GROUP + piece[0], 16), piece[1])
        number = STEPS[direction].index((distance, piece))
        return remote(
            weights[s].at[rows], weights[s].at[rows],
            ring_sem.at[0, s, direction, number], second_at[s](sign), r,
        )

    def gather_step(distance):
        for number in range(3 if distance < NEAR else 2):
            for direction in (0, 1):
                piece = PIECES[direction][number]
                for s in (0, 1):
                    if distance > 1:
                        got(("gather", s, direction, distance - 1, piece))
                    send(
                        ("gather", s, direction, distance, piece),
                        gather_copy(s, direction, distance, piece),
                    )

    gather_step(1)

    for load in loads[6:8]:
        load.wait()
    gain = gain_v[...].reshape(1, D)
    for h in range(1, REACH + 1):
        got(("token", h))
    work = dot(onehot(iota((HOME, WORK), 0) == work_index), tokens[...], 0, 0) + dot(
        onehot(iota((REACH * SLOT, WORK), 0) + HOME == work_index), arrived[...], 0, 0
    )
    work_s[...] = work.astype(BF16)
    centred = work - jnp.mean(work, axis=1, keepdims=True)
    inverse = lax.rsqrt(jnp.mean(centred * centred, axis=1, keepdims=True) + EPSILON)
    normed = centred * inverse
    normed_s[...] = normed
    inv_s[...] = jnp.broadcast_to(inverse, (WORK, 128))
    hidden_s[...] = (normed * gain).astype(BF16)

    gather_step(2)

    lane = iota((1, D), 1)
    outer = (lane * 6554) >> 20
    inner = lane - outer * GROUP
    middle = div20(inner)
    natural = middle * GROUP + outer * ROWS + (inner - middle * ROWS)
    for b in range(D // 256):
        perm[256 * b : 256 * (b + 1), :] = onehot(iota((256, D), 0) + 256 * b == natural)
    gather_step(3)
    both_s[0:WORK, :] = dot(hidden_s[...], perm[...]).astype(BF16)
    both_s[WORK : 2 * WORK, :] = dot(cotangent[...], perm[...]).astype(BF16)
    gather_step(4)
    both_t[...] = both_s[...].astype(F32).T.astype(BF16)
    hidden_t = hidden_s[...].astype(F32).T.astype(BF16)
    ids = jnp.broadcast_to(ident, (WORK, WORK))
    same_image = ids == ids.T
    for direction in (0, 1):
        for distance, piece in STEPS[direction]:
            if (distance + 1, piece) not in STEPS[direction]:
                for s in (0, 1):
                    got(("gather", s, direction, distance, piece))

    pa = dot(hidden_s[...], w0[...]).astype(BF16)
    pb = dot(both_s[...], w1[...]).astype(BF16)
    proj = jnp.concatenate([pa, pb[0:WORK, 0:128]], axis=1)
    scale = HEAD ** (-0.5)
    pieces, attended = [], []
    for j in (0, 1):
        q, k, v = (
            proj[:, 240 * j + HEAD * i : 240 * j + HEAD * (i + 1)] for i in range(3)
        )
        da = pb[WORK : 2 * WORK, 96 + HEAD * j : 96 + HEAD * (j + 1)]
        scores = jnp.where(same_image, dot(q, k, 1, 1) * scale, NEGATIVE)
        exponent = jnp.exp(scores - jnp.max(scores, axis=1, keepdims=True))
        probs = exponent / jnp.sum(exponent, axis=1, keepdims=True)
        probs_low = probs.astype(BF16)
        attended.append(dot(probs_low, v).astype(BF16))
        grad_probs = dot(da, v, 1, 1)
        grad_v = dot(probs_low, da, 0, 0).astype(BF16)
        grad_s = probs * (grad_probs - jnp.sum(probs * grad_probs, axis=1, keepdims=True))
        grad_s = (grad_s * scale).astype(BF16)
        pieces += [
            dot(grad_s, k).astype(BF16),
            dot(grad_s, q, 0, 0).astype(BF16),
            grad_v,
        ]
    mixed = jnp.concatenate(pieces + attended, axis=1)
    mix0 = mixed[:, 0:384]
    mix1 = mixed[:, 384:640]
    in_qkv = iota((WORK, 256), 1) < 96
    mix1_qkv = jnp.where(in_qkv, mix1, jnp.zeros_like(mix1))
    mix1_att = jnp.where(in_qkv, jnp.zeros_like(mix1), mix1)

    g0[...] = dot(hidden_t, mix0)
    g1[...] = dot(both_t[...], jnp.concatenate([mix1_qkv, mix1_att], axis=0))
    totals = (g0, g1)
    rings = (ring0, ring1)

    def sum_copy(s, direction, distance, piece):
        sign = 1 if direction == 0 else -1
        number = STEPS[direction].index((distance, piece))
        rows = pl.ds(*piece)
        return remote(
            rings[s].at[direction, distance, rows], rings[s].at[direction, distance - 1, rows],
            ring_sem.at[1, s, direction, number], second_at[s](sign), r,
        )

    def own_term(s, step, piece):
        at = around(second_pos[s], step, SIDE)
        return totals[s][pl.ds(pl.multiple_of(at * GROUP + piece[0], 16), piece[1]), :]

    def sum_step(distance):
        for number in range(3 if distance < NEAR else 2):
            for direction in (0, 1):
                piece = PIECES[direction][number]
                rows = pl.ds(*piece)
                sign = 1 if direction == 0 else -1
                for s in (0, 1):
                    total = own_term(s, sign * distance, piece)
                    if (distance + 1, piece) in STEPS[direction]:
                        got(("sum", s, direction, distance + 1, piece))
                        total = total + rings[s][direction, distance, rows].astype(F32)
                    rings[s][direction, distance, rows] = total.astype(BF16)
                    send(
                        ("sum", s, direction, distance, piece),
                        sum_copy(s, direction, distance, piece),
                    )

    def spread(kind, src, dst):
        for o in range(1, REP):
            rows = pl.ds(pl.multiple_of(at_rep(o) * 16, 16), 16)
            send(
                ("rep", kind, o),
                remote(src.at[rows], dst.at[r], rep_sem.at[kind, o], d, at_rep(o)),
            )

    my_rows = pl.ds(pl.multiple_of(r * 16, 16), 16)

    def all_got(kind):
        for o in range(1, REP):
            got(("rep", kind, o))

    def summed(kind, src, dst):
        dst[r] = src[my_rows, :]
        all_got(kind)
        total = dst[0].astype(F32)
        for i in range(1, REP):
            total = total + dst[i].astype(F32)
        return total

    def share(kind, ref):
        for o in range(1, REP):
            send(
                ("rep", kind, o),
                remote(ref.at[my_rows], ref.at[my_rows], rep_sem.at[kind, o], d, at_rep(o)),
            )

    sum_step(4)
    turned = dot(mix1_qkv, w1[...], 1, 1).astype(BF16)
    hid_p[...] = (dot(mix0, w0[...], 1, 1) + dot(turned, perm[...])).astype(BF16)
    spread(0, hid_p, hid_r)
    sum_step(3)
    turned = dot(mix1_att, w1[...], 1, 1).astype(BF16)
    lay_p[...] = dot(turned, perm[...]).astype(BF16)
    spread(1, lay_p, lay_r)

    back_index = spans_index(
        REACH * SLOT,
        [
            (w, jnp.where(hop == h, c, 0), o)
            for h in range(1, REACH + 1)
            for c, hop, o, s, w in senders[h]
        ],
    )
    home_index = spans_index(
        HOME, [(s, c, jnp.where(h == 0, o, WORK + w)) for c, h, o, s, w in mine]
    )

    sum_step(2)
    grad_hidden = summed(0, hid_p, hid_r)
    norm_rows = normed_s[my_rows, :]
    grad_normed = grad_hidden * gain
    correction = (
        grad_normed
        - jnp.mean(grad_normed, axis=1, keepdims=True)
        - norm_rows * jnp.mean(grad_normed * norm_rows, axis=1, keepdims=True)
    )
    work_g[my_rows, :] = (
        cotangent[my_rows, :].astype(F32) + inv_s[my_rows, 0:1] * correction
    ).astype(BF16)
    share(2, work_g)
    row_gain = jnp.sum(grad_hidden * norm_rows, axis=0, keepdims=True)
    gain_s[...] = jnp.zeros_like(gain_s)
    for t in range(D // 128):
        gain_s[0, t : t + 1, :] = row_gain[:, 128 * t : 128 * (t + 1)]

    gain_at = (
        (r, lambda o: (d, at_rep(o))),
        (y, lambda o: (at_y(o), r)),
        (z, lambda o: (at_z(o), r)),
    )

    def send_gain(level):
        me, peer = gain_at[level]
        for o in range(1, SIDE):
            send(
                ("gain", level, o),
                remote(gain_s.at[level], gain_r.at[level, me], sum_sem.at[level, o], *peer(o)),
            )
        gain_r[level, me] = gain_s[level]

    def sum_gain(level):
        for o in range(1, SIDE):
            got(("gain", level, o))
        total = gain_r[level, 0]
        for i in range(1, SIDE):
            total = total + gain_r[level, i]
        return total

    send_gain(0)

    sum_step(1)
    all_got(2)
    back_slots[...] = dot(
        onehot(iota((WORK, REACH * SLOT), 0) == back_index), work_g[...], 0, 0
    ).astype(BF16)
    for h in range(1, REACH + 1):
        rows = pl.ds(SLOT * (h - 1), SLOT)
        send(
            ("back", h),
            remote(back_slots.at[rows], back_arr.at[rows], token_sem.at[1, h - 1], at_dp(-h), r),
        )

    gain_s[1] = sum_gain(0)
    send_gain(1)

    projected = summed(1, lay_p, lay_r)
    lay_f[my_rows, :] = (work_s[my_rows, :].astype(F32) + projected).astype(BF16)
    share(3, lay_f)

    backs, heards = (back0, back1), (heard0, heard1)
    for s in (0, 1):
        for direction in (0, 1):
            for piece in PIECES[direction]:
                got(("sum", s, direction, 1, piece))
        total = own_term(s, 0, (0, GROUP))
        for direction in (0, 1):
            total = total + rings[s][direction, 0].astype(F32)
        dense = total.astype(BF16)
        spreadout = dot(puts[s][0], dense[:, 0:128])
        for t in range(1, TILES[s]):
            spreadout = spreadout + dot(puts[s][t], dense[:, 128 * t : 128 * (t + 1)])
        backs[s][...] = spreadout.astype(BF16).reshape(SIDE, PACK[s], 128)
        for o in range(1, SIDE):
            to = around(first_pos[s], o, SIDE)
            send(
                ("last", s, o),
                remote(backs[s].at[to], heards[s].at[first_pos[s]], part_sem.at[2 + s, o], first_at[s](o), r),
            )
        heards[s][first_pos[s]] = backs[s][first_pos[s]]

    gain_s[2] = sum_gain(1)
    send_gain(2)

    stores = []

    def store(src, dst):
        copy = pltpu.make_async_copy(src, dst, out_sem.at[len(stores)])
        copy.start()
        stores.append(copy)

    for h in range(1, REACH + 1):
        got(("back", h))
    input_o[...] = (
        dot(onehot(iota((WORK, HOME), 0) == home_index), work_g[...], 0, 0)
        + dot(onehot(iota((REACH * SLOT, HOME), 0) + WORK == home_index), back_arr[...], 0, 0)
    ).astype(BF16)
    store(input_o, input_h)
    all_got(3)
    store(lay_f, layer_h)

    tiles = []
    for s in (0, 1):
        for o in range(1, SIDE):
            got(("last", s, o))
        total = heards[s][0].astype(F32)
        for i in range(1, SIDE):
            total = total + heards[s][i].astype(F32)
        tiles += [total[PITCH * t : PITCH * t + ROWS, :] for t in range(TILES[s])]
    grad_qkv = jnp.concatenate(tiles[0:3] + [tiles[3][:, 0:96]], axis=1)
    gq_o[...] = grad_qkv
    go_o[...] = jnp.concatenate([tiles[3][:, 96:128], tiles[4]], axis=1)
    store(gq_o, gq_h)
    store(go_o, go_h)

    total = sum_gain(2)
    row = jnp.concatenate([total[t : t + 1, :] for t in range(D // 128)], axis=1)
    row = pltpu.roll(jnp.broadcast_to(row, (8, D)), lax.rem(D - ROWS * d, D), 1)
    gg_o[...] = row[0:1, 0:ROWS]
    store(gg_o, gg_h)

    for copy in stores:
        copy.wait()
    for copy in sent.values():
        copy.wait_send()


def finish(*refs):
    held, outs, rooms, sems = refs[0:5], refs[5:10], refs[10:15], refs[15]
    loads = [pltpu.make_async_copy(h, v, sems.at[0, i]) for i, (h, v) in enumerate(zip(held, rooms))]
    stores = [pltpu.make_async_copy(v, o, sems.at[1, i]) for i, (v, o) in enumerate(zip(rooms, outs))]
    for load in loads:
        load.start()
    for load, store in zip(loads, stores):
        load.wait()
        store.start()
    for store in stores:
        store.wait()


def body(tokens, cotangent, counts, hops, offsets, norm_gain, qkv_weight, out_weight):
    outside = pl.BlockSpec(memory_space=pl.ANY)
    dma = pltpu.SemaphoreType.DMA
    low = lambda *shape: pltpu.VMEM(shape, BF16)
    wide = lambda *shape: pltpu.VMEM(shape, F32)
    table = pltpu.SMEM((IMAGES, SIDE * SIDE), jnp.int32)
    shapes = (
        jax.ShapeDtypeStruct((WORK, D), BF16),
        jax.ShapeDtypeStruct((HOME, D), BF16),
        jax.ShapeDtypeStruct((ROWS, 480), F32),
        jax.ShapeDtypeStruct((ROWS, 160), F32),
        jax.ShapeDtypeStruct((1, ROWS), F32),
    )
    limit = 62 * 1024 * 1024
    outs = pl.pallas_call(
        kernel,
        out_shape=shapes,
        in_specs=[outside] * 8,
        out_specs=(outside,) * 5,
        scratch_shapes=[
            low(HOME, D), low(WORK, D), table, table, table, wide(D), low(ROWS, 480), low(ROWS, 160),
            low(HOME, D), wide(ROWS, 480), wide(ROWS, 160), wide(1, ROWS),
            wide(80, 128),
            low(PACK[0], 128), low(PACK[1], 128),
            low(SIDE, PACK[0], 128), low(SIDE, PACK[1], 128),
            low(D, 384), low(D, 256),
            low(3, GROUP, SIDE * PACK[0]), low(2, GROUP, SIDE * PACK[1]),
            low(3, SIDE * PACK[0], GROUP), low(2, SIDE * PACK[1], GROUP),
            low(D, D),
            low(REACH * SLOT, D), low(REACH * SLOT, D),
            low(WORK, D), wide(WORK, D), low(WORK, D), wide(WORK, 128),
            low(2 * WORK, D), low(D, 2 * WORK),
            wide(D, 384), wide(D, 256),
            low(2, NEAR + 1, GROUP, 384), low(2, NEAR + 1, GROUP, 256),
            low(SIDE, PACK[0], 128), low(SIDE, PACK[1], 128),
            low(SIDE, PACK[0], 128), low(SIDE, PACK[1], 128),
            low(WORK, D), low(REP, 16, D), low(WORK, D), low(REP, 16, D),
            low(WORK, D), low(WORK, D),
            low(REACH * SLOT, D), low(REACH * SLOT, D),
            wide(3, 16, 128), wide(3, SIDE, 16, 128),
            dma((4, SIDE, 2)),
            dma((2, 2, 2, len(STEPS[0]), 2)),
            dma((2, REACH, 2)),
            dma((4, REP, 2)),
            dma((3, SIDE, 2)),
            dma((8,)), dma((5,)),
        ],
        compiler_params=pltpu.CompilerParams(
            collective_id=0, has_side_effects=True, vmem_limit_bytes=limit
        ),
        name="layer",
    )(
        tokens, cotangent, counts.T, hops.T, offsets.T,
        norm_gain, qkv_weight, out_weight,
    )
    outs = pl.pallas_call(
        finish,
        out_shape=shapes,
        in_specs=[outside] * 5,
        out_specs=(outside,) * 5,
        scratch_shapes=[pltpu.VMEM(s.shape, s.dtype) for s in shapes] + [dma((2, 5))],
        compiler_params=pltpu.CompilerParams(vmem_limit_bytes=limit),
        name="finish",
    )(*outs)
    layer_out, input_grad, grad_qkv, grad_out, grad_gain = outs
    return (layer_out, input_grad, grad_qkv, grad_out, grad_gain.reshape(ROWS))


def solution(mesh):
    return jax.shard_map(
        body,
        mesh=mesh,
        in_specs=(P("dp", None), P("dp", None), P(), P(), P(), P(), P("dp", "rep"), P("dp", "rep")),
        out_specs=(P("dp", None), P("dp", None), P("dp", "rep"), P("dp", "rep"), P("dp")),
        check_vma=False,
    )
```

time: 90.2 us -> 78.3 us (0.87)
  local copies, waits for them, and re-layouts: 8.04 us -> 0 us
  Pallas kernels: 81.1 us -> 77.5 us
    unnamed x22 -> x0, local copies, waits for them, and re-layouts: 7.33 us -> none
    pallas_call x1 -> x2, Pallas kernels: 81.1 us -> 77.5 us  [the longest x1 75.6 us: body(): pl.pallas_call(kernel, out_shape=shapes, in_specs=[outside] * 8, out_spec...]
where the time goes in v2:
time: 78.3 us; the launch traced here: 78.2 us
  Pallas kernels  77.5 us (99%)
    pallas_call x1, Pallas kernels, body(): pl.pallas_call(kernel, out_shape=shapes, in_specs=[outside] * 8, out_spec...  75.6 us
    pallas_call x1, Pallas kernels, body(): pl.pallas_call(finish, out_shape=shapes, in_specs=[outside] * 5, out_spec...  1.98 us

profile of v2, /device:TPU:1, one launch (start us, length us, event | category | flops | bytes accessed | tf_op | source)
XLA Modules:
  0.0 78.2 jit_solution(2443609436819007953)
XLA Ops:
  0.6 75.6 %layer.1 = (bf16[128,1280]{1,0:T(8,128)(2,1)}, bf16[176,1280]{1,0:T(8,128)(2,1)}, f32[20,480]{1,0:T(8,128)}, f32[20,160]{1,0:T(8,128)}, f32[1,20]{1,0:T(1,128)}) custom-call(bf16[176,1280]{1,0:T(8,128)(2,1)} %tokens_h.1, bf16[128,1280]{1,0:T(8,128)(2,1)} %cotangent_h.1, s32[8,64]{1,0:T(8,128)} %bitcast.4, s32[8,64]{1,0:T(8,128)} %bitcast.5, ...), custom_call_target="tpu_custom_call" | custom-call | tf_op jit(solution)/shard_map/layer/pallas_call | solution.py:578
  76.2 2.0 %finish.1 = (bf16[128,1280]{1,0:T(8,128)(2,1)}, bf16[176,1280]{1,0:T(8,128)(2,1)}, f32[20,480]{1,0:T(8,128)}, f32[20,160]{1,0:T(8,128)}, f32[1,20]{1,0:T(1,128)}) custom-call(bf16[128,1280]{1,0:T(8,128)(2,1)} %get-tuple-element.15.refs_0_, bf16[176,1280]{1,0:T(8,128)(2,1)} %get-tuple-element.16.refs_1_, f32[20,480]{1,0:T(8,128)} %get-tuple-element.17.refs_2_, ...), custom_call_target="tpu_custom_call" | custom-call | tf_op jit(solution)/shard_map/finish/pallas_call | solution.py:619

commit v3 on v2

--- a/solution.py
+++ b/solution.py
@@ -23,11 +23,12 @@
 IMAGES = 8
 EPSILON = 1e-06
 NEGATIVE = -1e30
-PITCH = 24
+XS = 4
+COLS = D // 2
 
 TILES = (3, 2)
 FIRST = (0, 384)
-PACK = (80, 48)
+PACK = (64, 48)
 
 
 def dot(a, b, ca=1, cb=0):
@@ -95,13 +96,15 @@
     stage, own0, own1, parts0, parts1, w0, w1, pick0, pick1, put0, put1, perm,
     slots, arrived, work_s, normed_s, hidden_s, inv_s, both_s, both_t,
     g0, g1, ring0, ring1, back0, back1, heard0, heard1,
-    hid_p, hid_r, lay_p, lay_r, work_g, lay_f, back_slots, back_arr, gain_s, gain_r,
-    part_sem, ring_sem, token_sem, rep_sem, sum_sem, in_sem, out_sem,
+    hid_p, hid_h, hid_x, hid_r, lay_p, lay_h, lay_x, lay_r, work_g, lay_f, back_slots, back_arr, gain_s, gain_r,
+    part_sem, ring_sem, token_sem, x_sem, pair_sem, sum_sem, in_sem, out_sem,
 ):
     d = lax.axis_index("dp")
     r = lax.axis_index("rep")
     y = d // SIDE
     z = d % SIDE
+    x = r // 2
+    core = r % 2
 
     def around(value, step, count):
         return lax.rem(value + (step + count), count)
@@ -117,6 +120,11 @@
 
     def at_rep(step):
         return around(r, step, REP)
+
+    def at_x(step):
+        return around(x, step, XS) * 2 + core
+
+    other_core = x * 2 + 1 - core
 
     sent = {}
 
@@ -132,6 +140,9 @@
 
     def got(key):
         sent[key].wait_recv()
+
+    def pair(number, src, dst):
+        send(("pair", number), remote(src, dst, pair_sem.at[number], d, other_core))
 
     barrier = pltpu.get_barrier_semaphore()
     partners = (
@@ -161,10 +172,10 @@
     wide = qkv_w[...].astype(F32)
     wide_out = out_w[...].astype(F32)
     for t in range(3):
-        stage[PITCH * t : PITCH * t + ROWS, :] = wide[:, 128 * t : 128 * (t + 1)]
+        stage[ROWS * t : ROWS * t + ROWS, :] = wide[:, 128 * t : 128 * (t + 1)]
     own0[...] = stage[0 : PACK[0], :].astype(BF16)
     stage[0:ROWS, :] = jnp.concatenate([wide[:, 384:480], wide_out[:, 0:32]], axis=1)
-    stage[PITCH : PITCH + ROWS, :] = wide_out[:, 32:160]
+    stage[ROWS : ROWS + ROWS, :] = wide_out[:, 32:160]
     own1[...] = stage[0 : PACK[1], :].astype(BF16)
 
     pl.semaphore_wait(barrier, len(partners))
@@ -187,14 +198,16 @@
     out_index = spans_index(
         REACH * SLOT, [(w, jnp.where(h > 0, c, 0), s) for c, h, o, s, w in mine]
     )
-    slots[...] = dot(
+    moved = dot(
         onehot(iota((HOME, REACH * SLOT), 0) == out_index), tokens[...], 0, 0
     ).astype(BF16)
+    for half in (0, 1):
+        slots[half] = moved[:, COLS * half : COLS * (half + 1)]
     for h in range(1, REACH + 1):
         rows = pl.ds(SLOT * (h - 1), SLOT)
         send(
             ("token", h),
-            remote(slots.at[rows], arrived.at[rows], token_sem.at[0, h - 1], at_dp(h), r),
+            remote(slots.at[core, rows], arrived.at[core, rows], token_sem.at[0, h - 1], at_dp(h), r),
         )
     for s in (0, 1):
         parts[s][first_pos[s]] = own[s][...]
@@ -203,15 +216,15 @@
     for s in (0, 1):
         rows = SIDE * PACK[s]
         lane = iota((1, rows), 1)
-        block = (lane * 820) >> 16 if s == 0 else (lane * 1366) >> 16
+        block = lane >> 6 if s == 0 else (lane * 1366) >> 16
         inner = lane - block * PACK[s]
         dense = iota((1, GROUP), 1)
         owner = div20(dense)
         for t in range(TILES[s]):
-            row = inner - PITCH * t
+            row = inner - ROWS * t
             target = jnp.where((row >= 0) & (row < ROWS), block * ROWS + row, -1)
             picks[s][t] = onehot(iota((GROUP, rows), 0) == target)
-            source = dense + owner * (PACK[s] - ROWS) + PITCH * t
+            source = dense + owner * (PACK[s] - ROWS) + ROWS * t
             puts[s][t] = onehot(iota((rows, GROUP), 0) == source)
 
     work_spans, work_ids = [], []
@@ -228,6 +241,14 @@
             ident = jnp.where(inside, float(h * IMAGES + j), ident)
     work_index = spans_index(WORK, work_spans)
 
+    lane = iota((1, D), 1)
+    outer = (lane * 6554) >> 20
+    inner = lane - outer * GROUP
+    middle = div20(inner)
+    natural = middle * GROUP + outer * ROWS + (inner - middle * ROWS)
+    for b in range(D // 256):
+        perm[256 * b : 256 * (b + 1), :] = onehot(iota((256, D), 0) + 256 * b == natural)
+
     for o in range(1, SIDE):
         for s in (0, 1):
             got(("part", s, o))
@@ -264,13 +285,19 @@
 
     gather_step(1)
 
+    gather_step(2)
+    for h in range(1, REACH + 1):
+        got(("token", h))
+    pair(0, arrived.at[core], arrived.at[core])
+    gather_step(3)
+
     for load in loads[6:8]:
         load.wait()
     gain = gain_v[...].reshape(1, D)
-    for h in range(1, REACH + 1):
-        got(("token", h))
+    got(("pair", 0))
+    received = jnp.concatenate([arrived[0], arrived[1]], axis=1)
     work = dot(onehot(iota((HOME, WORK), 0) == work_index), tokens[...], 0, 0) + dot(
-        onehot(iota((REACH * SLOT, WORK), 0) + HOME == work_index), arrived[...], 0, 0
+        onehot(iota((REACH * SLOT, WORK), 0) + HOME == work_index), received, 0, 0
     )
     work_s[...] = work.astype(BF16)
     centred = work - jnp.mean(work, axis=1, keepdims=True)
@@ -279,20 +306,10 @@
     normed_s[...] = normed
     inv_s[...] = jnp.broadcast_to(inverse, (WORK, 128))
     hidden_s[...] = (normed * gain).astype(BF16)
-
-    gather_step(2)
-
-    lane = iota((1, D), 1)
-    outer = (lane * 6554) >> 20
-    inner = lane - outer * GROUP
-    middle = div20(inner)
-    natural = middle * GROUP + outer * ROWS + (inner - middle * ROWS)
-    for b in range(D // 256):
-        perm[256 * b : 256 * (b + 1), :] = onehot(iota((256, D), 0) + 256 * b == natural)
-    gather_step(3)
+    gather_step(4)
+
     both_s[0:WORK, :] = dot(hidden_s[...], perm[...]).astype(BF16)
     both_s[WORK : 2 * WORK, :] = dot(cotangent[...], perm[...]).astype(BF16)
-    gather_step(4)
     both_t[...] = both_s[...].astype(F32).T.astype(BF16)
     hidden_t = hidden_s[...].astype(F32).T.astype(BF16)
     ids = jnp.broadcast_to(ident, (WORK, WORK))
@@ -369,43 +386,56 @@
                         sum_copy(s, direction, distance, piece),
                     )
 
-    def spread(kind, src, dst):
-        for o in range(1, REP):
-            rows = pl.ds(pl.multiple_of(at_rep(o) * 16, 16), 16)
+    block = core * XS + x
+    my_rows = pl.ds(pl.multiple_of(block * 16, 16), 16)
+    my_half = pl.ds(pl.multiple_of(core * 64, 64), 64)
+    other_half = pl.ds(pl.multiple_of(64 - core * 64, 64), 64)
+
+    def pair_sum(kind, src, theirs, staged):
+        got(("pair", 1 + kind))
+        total = src[my_half, :].astype(F32) + theirs[...].astype(F32)
+        staged[...] = total.astype(BF16).reshape(XS, 16, D)
+
+    def spread(kind, staged, dst):
+        for o in range(1, XS):
             send(
-                ("rep", kind, o),
-                remote(src.at[rows], dst.at[r], rep_sem.at[kind, o], d, at_rep(o)),
+                ("x", kind, o),
+                remote(staged.at[around(x, o, XS)], dst.at[x], x_sem.at[kind, o], d, at_x(o)),
             )
-
-    my_rows = pl.ds(pl.multiple_of(r * 16, 16), 16)
-
-    def all_got(kind):
-        for o in range(1, REP):
-            got(("rep", kind, o))
-
-    def summed(kind, src, dst):
-        dst[r] = src[my_rows, :]
-        all_got(kind)
+        dst[x] = staged[x]
+
+    def summed(kind, dst):
+        for o in range(1, XS):
+            got(("x", kind, o))
         total = dst[0].astype(F32)
-        for i in range(1, REP):
+        for i in range(1, XS):
             total = total + dst[i].astype(F32)
         return total
 
     def share(kind, ref):
-        for o in range(1, REP):
+        for o in range(1, XS):
             send(
-                ("rep", kind, o),
-                remote(ref.at[my_rows], ref.at[my_rows], rep_sem.at[kind, o], d, at_rep(o)),
+                ("x", kind, o),
+                remote(ref.at[my_rows], ref.at[my_rows], x_sem.at[kind, o], d, at_x(o)),
             )
+
+    def share_half(kind, ref):
+        for o in range(1, XS):
+            got(("x", kind, o))
+        pair(1 + kind, ref.at[my_half], ref.at[my_half])
 
     sum_step(4)
     turned = dot(mix1_qkv, w1[...], 1, 1).astype(BF16)
     hid_p[...] = (dot(mix0, w0[...], 1, 1) + dot(turned, perm[...])).astype(BF16)
-    spread(0, hid_p, hid_r)
-    sum_step(3)
+    pair(1, hid_p.at[other_half], hid_h)
     turned = dot(mix1_att, w1[...], 1, 1).astype(BF16)
     lay_p[...] = dot(turned, perm[...]).astype(BF16)
-    spread(1, lay_p, lay_r)
+    pair(2, lay_p.at[other_half], lay_h)
+    pair_sum(0, hid_p, hid_h, hid_x)
+    spread(0, hid_x, hid_r)
+    sum_step(3)
+    pair_sum(1, lay_p, lay_h, lay_x)
+    spread(1, lay_x, lay_r)
 
     back_index = spans_index(
         REACH * SLOT,
@@ -419,8 +449,7 @@
         HOME, [(s, c, jnp.where(h == 0, o, WORK + w)) for c, h, o, s, w in mine]
     )
 
-    sum_step(2)
-    grad_hidden = summed(0, hid_p, hid_r)
+    grad_hidden = summed(0, hid_r)
     norm_rows = normed_s[my_rows, :]
     grad_normed = grad_hidden * gain
     correction = (
@@ -462,24 +491,33 @@
 
     send_gain(0)
 
-    sum_step(1)
-    all_got(2)
-    back_slots[...] = dot(
+    sum_step(2)
+    share_half(2, work_g)
+    projected = summed(1, lay_r)
+    lay_f[my_rows, :] = (work_s[my_rows, :].astype(F32) + projected).astype(BF16)
+    share(3, lay_f)
+    got(("pair", 3))
+    moved = dot(
         onehot(iota((WORK, REACH * SLOT), 0) == back_index), work_g[...], 0, 0
     ).astype(BF16)
+    for half in (0, 1):
+        back_slots[half] = moved[:, COLS * half : COLS * (half + 1)]
     for h in range(1, REACH + 1):
         rows = pl.ds(SLOT * (h - 1), SLOT)
         send(
             ("back", h),
-            remote(back_slots.at[rows], back_arr.at[rows], token_sem.at[1, h - 1], at_dp(-h), r),
+            remote(back_slots.at[core, rows], back_arr.at[core, rows], token_sem.at[1, h - 1], at_dp(-h), r),
         )
-
     gain_s[1] = sum_gain(0)
     send_gain(1)
 
-    projected = summed(1, lay_p, lay_r)
-    lay_f[my_rows, :] = (work_s[my_rows, :].astype(F32) + projected).astype(BF16)
-    share(3, lay_f)
+    sum_step(1)
+    share_half(3, lay_f)
+    for h in range(1, REACH + 1):
+        got(("back", h))
+    pair(5, back_arr.at[core], back_arr.at[core])
+    gain_s[2] = sum_gain(1)
+    send_gain(2)
 
     backs, heards = (back0, back1), (heard0, heard1)
     for s in (0, 1):
@@ -502,9 +540,6 @@
             )
         heards[s][first_pos[s]] = backs[s][first_pos[s]]
 
-    gain_s[2] = sum_gain(1)
-    send_gain(2)
-
     stores = []
 
     def store(src, dst):
@@ -512,14 +547,14 @@
         copy.start()
         stores.append(copy)
 
-    for h in range(1, REACH + 1):
-        got(("back", h))
+    got(("pair", 5))
+    received = jnp.concatenate([back_arr[0], back_arr[1]], axis=1)
     input_o[...] = (
         dot(onehot(iota((WORK, HOME), 0) == home_index), work_g[...], 0, 0)
-        + dot(onehot(iota((REACH * SLOT, HOME), 0) + WORK == home_index), back_arr[...], 0, 0)
+        + dot(onehot(iota((REACH * SLOT, HOME), 0) + WORK == home_index), received, 0, 0)
     ).astype(BF16)
     store(input_o, input_h)
-    all_got(3)
+    got(("pair", 4))
     store(lay_f, layer_h)
 
     tiles = []
@@ -529,7 +564,7 @@
         total = heards[s][0].astype(F32)
         for i in range(1, SIDE):
             total = total + heards[s][i].astype(F32)
-        tiles += [total[PITCH * t : PITCH * t + ROWS, :] for t in range(TILES[s])]
+        tiles += [total[ROWS * t : ROWS * t + ROWS, :] for t in range(TILES[s])]
     grad_qkv = jnp.concatenate(tiles[0:3] + [tiles[3][:, 0:96]], axis=1)
     gq_o[...] = grad_qkv
     go_o[...] = jnp.concatenate([tiles[3][:, 96:128], tiles[4]], axis=1)
@@ -583,28 +618,29 @@
         scratch_shapes=[
             low(HOME, D), low(WORK, D), table, table, table, wide(D), low(ROWS, 480), low(ROWS, 160),
             low(HOME, D), wide(ROWS, 480), wide(ROWS, 160), wide(1, ROWS),
-            wide(80, 128),
+            wide(64, 128),
             low(PACK[0], 128), low(PACK[1], 128),
             low(SIDE, PACK[0], 128), low(SIDE, PACK[1], 128),
             low(D, 384), low(D, 256),
             low(3, GROUP, SIDE * PACK[0]), low(2, GROUP, SIDE * PACK[1]),
             low(3, SIDE * PACK[0], GROUP), low(2, SIDE * PACK[1], GROUP),
             low(D, D),
-            low(REACH * SLOT, D), low(REACH * SLOT, D),
+            low(2, REACH * SLOT, COLS), low(2, REACH * SLOT, COLS),
             low(WORK, D), wide(WORK, D), low(WORK, D), wide(WORK, 128),
             low(2 * WORK, D), low(D, 2 * WORK),
             wide(D, 384), wide(D, 256),
             low(2, NEAR + 1, GROUP, 384), low(2, NEAR + 1, GROUP, 256),
             low(SIDE, PACK[0], 128), low(SIDE, PACK[1], 128),
             low(SIDE, PACK[0], 128), low(SIDE, PACK[1], 128),
-            low(WORK, D), low(REP, 16, D), low(WORK, D), low(REP, 16, D),
+            low(WORK, D), low(64, D), low(XS, 16, D), low(XS, 16, D),
+            low(WORK, D), low(64, D), low(XS, 16, D), low(XS, 16, D),
             low(WORK, D), low(WORK, D),
-            low(REACH * SLOT, D), low(REACH * SLOT, D),
+            low(2, REACH * SLOT, COLS), low(2, REACH * SLOT, COLS),
             wide(3, 16, 128), wide(3, SIDE, 16, 128),
             dma((4, SIDE, 2)),
             dma((2, 2, 2, len(STEPS[0]), 2)),
             dma((2, REACH, 2)),
-            dma((4, REP, 2)),
+            dma((4, XS, 2)), dma((6, 2)),
             dma((3, SIDE, 2)),
             dma((8,)), dma((5,)),
         ],

time: 78.3 us -> 73 us (0.932)
  Pallas kernels: 77.5 us -> 72.2 us
    pallas_call x1, Pallas kernels: 75.6 us -> 70.2 us  [body(): pl.pallas_call(kernel, out_shape=shapes, in_specs=[outside] * 8, out_spec...]
where the time goes in v3:
time: 73 us; the launch traced here: 72.8 us
  Pallas kernels  72.2 us (99%)
    pallas_call x1, Pallas kernels, body(): pl.pallas_call(kernel, out_shape=shapes, in_specs=[outside] * 8, out_spec...  70.2 us
    pallas_call x1, Pallas kernels, body(): pl.pallas_call(finish, out_shape=shapes, in_specs=[outside] * 5, out_spec...  1.98 us

profile of v3, /device:TPU:1, one launch (start us, length us, event | category | flops | bytes accessed | tf_op | source)
XLA Modules:
  0.0 72.8 jit_solution(8619339339992094270)
XLA Ops:
  0.6 70.2 %layer.1 = (bf16[128,1280]{1,0:T(8,128)(2,1)}, bf16[176,1280]{1,0:T(8,128)(2,1)}, f32[20,480]{1,0:T(8,128)}, f32[20,160]{1,0:T(8,128)}, f32[1,20]{1,0:T(1,128)}) custom-call(bf16[176,1280]{1,0:T(8,128)(2,1)} %tokens_h.1, bf16[128,1280]{1,0:T(8,128)(2,1)} %cotangent_h.1, s32[8,64]{1,0:T(8,128)} %bitcast.4, s32[8,64]{1,0:T(8,128)} %bitcast.5, ...), custom_call_target="tpu_custom_call" | custom-call | tf_op jit(solution)/shard_map/layer/pallas_call | solution.py:613
  70.8 2.0 %finish.1 = (bf16[128,1280]{1,0:T(8,128)(2,1)}, bf16[176,1280]{1,0:T(8,128)(2,1)}, f32[20,480]{1,0:T(8,128)}, f32[20,160]{1,0:T(8,128)}, f32[1,20]{1,0:T(1,128)}) custom-call(bf16[128,1280]{1,0:T(8,128)(2,1)} %get-tuple-element.15.refs_0_, bf16[176,1280]{1,0:T(8,128)(2,1)} %get-tuple-element.16.refs_1_, f32[20,480]{1,0:T(8,128)} %get-tuple-element.17.refs_2_, ...), custom_call_target="tpu_custom_call" | custom-call | tf_op jit(solution)/shard_map/finish/pallas_call | solution.py:655

commit v4 on v3

--- a/solution.py
+++ b/solution.py
@@ -125,6 +125,10 @@
         return around(x, step, XS) * 2 + core
 
     other_core = x * 2 + 1 - core
+    block = core * XS + x
+    my_rows = pl.ds(pl.multiple_of(block * 16, 16), 16)
+    my_half = pl.ds(pl.multiple_of(core * 64, 64), 64)
+    other_half = pl.ds(pl.multiple_of(64 - core * 64, 64), 64)
 
     sent = {}
 
@@ -351,6 +355,10 @@
     mix1_qkv = jnp.where(in_qkv, mix1, jnp.zeros_like(mix1))
     mix1_att = jnp.where(in_qkv, jnp.zeros_like(mix1), mix1)
 
+    turned = dot(mix1_qkv, w1[...], 1, 1).astype(BF16)
+    hid_p[...] = (dot(mix0, w0[...], 1, 1) + dot(turned, perm[...])).astype(BF16)
+    pair(1, hid_p.at[other_half], hid_h)
+
     g0[...] = dot(hidden_t, mix0)
     g1[...] = dot(both_t[...], jnp.concatenate([mix1_qkv, mix1_att], axis=0))
     totals = (g0, g1)
@@ -386,11 +394,6 @@
                         sum_copy(s, direction, distance, piece),
                     )
 
-    block = core * XS + x
-    my_rows = pl.ds(pl.multiple_of(block * 16, 16), 16)
-    my_half = pl.ds(pl.multiple_of(core * 64, 64), 64)
-    other_half = pl.ds(pl.multiple_of(64 - core * 64, 64), 64)
-
     def pair_sum(kind, src, theirs, staged):
         got(("pair", 1 + kind))
         total = src[my_half, :].astype(F32) + theirs[...].astype(F32)
@@ -425,14 +428,11 @@
         pair(1 + kind, ref.at[my_half], ref.at[my_half])
 
     sum_step(4)
-    turned = dot(mix1_qkv, w1[...], 1, 1).astype(BF16)
-    hid_p[...] = (dot(mix0, w0[...], 1, 1) + dot(turned, perm[...])).astype(BF16)
-    pair(1, hid_p.at[other_half], hid_h)
+    pair_sum(0, hid_p, hid_h, hid_x)
+    spread(0, hid_x, hid_r)
     turned = dot(mix1_att, w1[...], 1, 1).astype(BF16)
     lay_p[...] = dot(turned, perm[...]).astype(BF16)
     pair(2, lay_p.at[other_half], lay_h)
-    pair_sum(0, hid_p, hid_h, hid_x)
-    spread(0, hid_x, hid_r)
     sum_step(3)
     pair_sum(1, lay_p, lay_h, lay_x)
     spread(1, lay_x, lay_r)
@@ -492,10 +492,13 @@
     send_gain(0)
 
     sum_step(2)
-    share_half(2, work_g)
     projected = summed(1, lay_r)
     lay_f[my_rows, :] = (work_s[my_rows, :].astype(F32) + projected).astype(BF16)
     share(3, lay_f)
+    sum_step(1)
+    share_half(2, work_g)
+    gain_s[1] = sum_gain(0)
+    send_gain(1)
     got(("pair", 3))
     moved = dot(
         onehot(iota((WORK, REACH * SLOT), 0) == back_index), work_g[...], 0, 0
@@ -508,16 +511,6 @@
             ("back", h),
             remote(back_slots.at[core, rows], back_arr.at[core, rows], token_sem.at[1, h - 1], at_dp(-h), r),
         )
-    gain_s[1] = sum_gain(0)
-    send_gain(1)
-
-    sum_step(1)
-    share_half(3, lay_f)
-    for h in range(1, REACH + 1):
-        got(("back", h))
-    pair(5, back_arr.at[core], back_arr.at[core])
-    gain_s[2] = sum_gain(1)
-    send_gain(2)
 
     backs, heards = (back0, back1), (heard0, heard1)
     for s in (0, 1):
@@ -540,6 +533,9 @@
             )
         heards[s][first_pos[s]] = backs[s][first_pos[s]]
 
+    share_half(3, lay_f)
+    gain_s[2] = sum_gain(1)
+    send_gain(2)
     stores = []
 
     def store(src, dst):
@@ -547,6 +543,9 @@
         copy.start()
         stores.append(copy)
 
+    for h in range(1, REACH + 1):
+        got(("back", h))
+    pair(5, back_arr.at[core], back_arr.at[core])
     got(("pair", 5))
     received = jnp.concatenate([back_arr[0], back_arr[1]], axis=1)
     input_o[...] = (

time: 73 us -> 70.4 us (0.964)
  Pallas kernels: 72.2 us -> 69.3 us
    pallas_call x1, Pallas kernels: 70.2 us -> 67.3 us  [body(): pl.pallas_call(kernel, out_shape=shapes, in_specs=[outside] * 8, out_spec...]
where the time goes in v4:
time: 70.4 us; the launch traced here: 70 us
  Pallas kernels  69.3 us (98%)
    pallas_call x1, Pallas kernels, body(): pl.pallas_call(kernel, out_shape=shapes, in_specs=[outside] * 8, out_spec...  67.3 us
    pallas_call x1, Pallas kernels, body(): pl.pallas_call(finish, out_shape=shapes, in_specs=[outside] * 5, out_spec...  1.98 us

profile of v4, /device:TPU:1, one launch (start us, length us, event | category | flops | bytes accessed | tf_op | source)
XLA Modules:
  0.0 70.0 jit_solution(9176066829105854196)
XLA Ops:
  0.6 67.3 %layer.1 = (bf16[128,1280]{1,0:T(8,128)(2,1)}, bf16[176,1280]{1,0:T(8,128)(2,1)}, f32[20,480]{1,0:T(8,128)}, f32[20,160]{1,0:T(8,128)}, f32[1,20]{1,0:T(1,128)}) custom-call(bf16[176,1280]{1,0:T(8,128)(2,1)} %tokens_h.1, bf16[128,1280]{1,0:T(8,128)(2,1)} %cotangent_h.1, s32[8,64]{1,0:T(8,128)} %bitcast.4, s32[8,64]{1,0:T(8,128)} %bitcast.5, ...), custom_call_target="tpu_custom_call" | custom-call | tf_op jit(solution)/shard_map/layer/pallas_call | solution.py:612
  68.0 2.0 %finish.1 = (bf16[128,1280]{1,0:T(8,128)(2,1)}, bf16[176,1280]{1,0:T(8,128)(2,1)}, f32[20,480]{1,0:T(8,128)}, f32[20,160]{1,0:T(8,128)}, f32[1,20]{1,0:T(1,128)}) custom-call(bf16[128,1280]{1,0:T(8,128)(2,1)} %get-tuple-element.15.refs_0_, bf16[176,1280]{1,0:T(8,128)(2,1)} %get-tuple-element.16.refs_1_, f32[20,480]{1,0:T(8,128)} %get-tuple-element.17.refs_2_, ...), custom_call_target="tpu_custom_call" | custom-call | tf_op jit(solution)/shard_map/finish/pallas_call | solution.py:654
